TPU v7x, 128 devices: a whole 4x4x4 slice. The times are simulated.
128 devices in a mesh: node: 16 (over z_hi, y, core), local: 8 (over x, z_lo).
Axes of the slice: x: 4, y: 4, z: 4 (z_hi: 2, z_lo: 2; z = z_hi * 2 + z_lo), core: 2. Of those that a mesh axis runs over, the one named last changes fastest.
Arguments:
- tokens: bfloat16 [16384, 2048], P(('node', 'local')), may hold values from -6 to 6
- out_grad: bfloat16 [16384, 2048], P(('node', 'local')), may hold values from -6 to 6
- expert_ids: int32 [16384, 8], P(('node', 'local')), may hold values from 0 to 127, all different within a row; in each aligned block of 128 rows (0 to 127, 128 to 255, ...) at most 9 rows name the same one
- gates: bfloat16 [16384, 8], P(('node', 'local')), may hold values from 0.019897461 to 0.3984375
- gate_weight: bfloat16 [128, 2048, 768], P(('node', 'local')), may hold values from -0.125 to 0.125
- up_weight: bfloat16 [128, 2048, 768], P(('node', 'local')), may hold values from -0.125 to 0.125
- down_weight: bfloat16 [128, 768, 2048], P(('node', 'local')), may hold values from -0.21875 to 0.21875
Outputs:
- input_grad: bfloat16 [16384, 2048], P(('node', 'local'))
- gate_weight_grad: bfloat16 [128, 2048, 768], P(('node', 'local'))
- up_weight_grad: bfloat16 [128, 2048, 768], P(('node', 'local'))
- down_weight_grad: bfloat16 [128, 768, 2048], P(('node', 'local'))
Inputs may be any that keep to these rules, and one draw needn't show every extreme that they name: `expert_ids`: each row names 8 different experts. Among the tokens of one device no expert is named more than 9 times, and in every draw some expert is named exactly 9 times by the tokens of some device.
All inputs are finite; a program needn't handle non-finite values.
Results may differ from a plain program's by a relative error of at most 0.0065.
Values may be sent and summed in bfloat16 or wider, within the bound.
A program may use at most 192 MiB of HBM per device.

v0:
```python
import jax
import jax.numpy as jnp
from jax import lax
from jax.sharding import PartitionSpec as P


def body(tokens, out_grad, expert_ids, gates, gate_weight, up_weight, down_weight):
    tok_count, model_width = tokens.shape
    top_count = expert_ids.shape[1]
    node_count = lax.axis_size("node")
    local_count = lax.axis_size("local")
    groups = node_count * local_count
    exp_local = gate_weight.shape[0]
    experts = exp_local * groups
    slot_cap = max(2, tok_count * top_count * 9 // (8 * experts))
    pair_count = tok_count * top_count
    flat_ids = expert_ids.reshape(pair_count)
    onehot = (flat_ids[:, None] == jnp.arange(experts, dtype=jnp.int32)[None, :]).astype(jnp.int32)
    earlier = jnp.cumsum(onehot, axis=0) - onehot
    slot_index = jnp.sum(earlier * onehot, axis=1)
    target = flat_ids * slot_cap + slot_index
    owners = jnp.full((experts * slot_cap,), pair_count, jnp.int32)
    owners = owners.at[target].set(jnp.arange(pair_count, dtype=jnp.int32))
    zero_row = jnp.zeros((1, model_width), jnp.bfloat16)
    token_pad = jnp.concatenate([tokens, zero_row], axis=0)
    scaled = (
        gates.astype(jnp.float32)[:, :, None] * out_grad.astype(jnp.float32)[:, None, :]
    ).astype(jnp.bfloat16)
    scaled_pad = jnp.concatenate([scaled.reshape(pair_count, model_width), zero_row], axis=0)
    sent_rows = token_pad[owners // top_count].reshape(groups, exp_local, slot_cap, model_width)
    sent_grad = scaled_pad[owners].reshape(groups, exp_local, slot_cap, model_width)
    got_rows, got_grad = (
        lax.all_to_all(sent_rows, ("node", "local"), split_axis=0, concat_axis=0, tiled=True),
        lax.all_to_all(sent_grad, ("node", "local"), split_axis=0, concat_axis=0, tiled=True),
    )
    gate_pre = jnp.einsum(
        "secd,edf->secf", got_rows, gate_weight, preferred_element_type=jnp.float32
    )
    up_pre = jnp.einsum("secd,edf->secf", got_rows, up_weight, preferred_element_type=jnp.float32)
    logistic = jax.nn.sigmoid(gate_pre)
    silu_gate = gate_pre * logistic
    hidden = (silu_gate * up_pre).astype(jnp.bfloat16)
    hidden_grad = jnp.einsum(
        "secd,efd->secf", got_grad, down_weight, preferred_element_type=jnp.float32
    )
    up_grad = (hidden_grad * silu_gate).astype(jnp.bfloat16)
    gate_grad = (hidden_grad * up_pre * logistic * (1.0 + gate_pre * (1.0 - logistic))).astype(
        jnp.bfloat16
    )
    slot_grad = (
        jnp.einsum("secf,edf->secd", gate_grad, gate_weight, preferred_element_type=jnp.float32)
        + jnp.einsum("secf,edf->secd", up_grad, up_weight, preferred_element_type=jnp.float32)
    ).astype(jnp.bfloat16)
    returned = lax.all_to_all(slot_grad, ("node", "local"), split_axis=0, concat_axis=0, tiled=True)
    down_weight_grad = jnp.einsum(
        "secf,secd->efd", hidden, got_grad, preferred_element_type=jnp.float32
    ).astype(jnp.bfloat16)
    gate_weight_grad = jnp.einsum(
        "secd,secf->edf", got_rows, gate_grad, preferred_element_type=jnp.float32
    ).astype(jnp.bfloat16)
    up_weight_grad = jnp.einsum(
        "secd,secf->edf", got_rows, up_grad, preferred_element_type=jnp.float32
    ).astype(jnp.bfloat16)
    back_rows = returned.reshape(experts * slot_cap, model_width)
    pair_rows = back_rows[target].reshape(tok_count, top_count, model_width)
    input_grad = jnp.sum(pair_rows.astype(jnp.float32), axis=1).astype(jnp.bfloat16)
    return (input_grad, gate_weight_grad, up_weight_grad, down_weight_grad)


def solution(mesh):
    in_specs = (
        P(("node", "local"), None),
        P(("node", "local"), None),
        P(("node", "local"), None),
        P(("node", "local"), None),
        P(("node", "local"), None, None),
        P(("node", "local"), None, None),
        P(("node", "local"), None, None),
    )
    out_specs = (
        P(("node", "local"), None),
        P(("node", "local"), None, None),
        P(("node", "local"), None, None),
        P(("node", "local"), None, None),
    )
    return jax.shard_map(body, mesh=mesh, in_specs=in_specs, out_specs=out_specs, check_vma=False)
```

profile of v0, /device:TPU:13, one launch (start us, length us, event | category | flops | bytes accessed | tf_op | source)
XLA Modules:
  0.0 432.9 jit_solution(1169699881106204322)
XLA Ops:
  0.6 0.0 copy-start
  0.6 0.8 broadcast_multiply_fusion
  1.5 0.9 copy.28
  2.4 0.1 eq.29
  2.5 0.1 eq.25
  2.6 0.1 copy.27
  2.7 0.1 mul.68
  2.8 0.1 copy.30
  2.9 0.2 fusion.45
  3.1 0.0 copy-start.2
  3.1 0.8 copy-done.2
  3.9 1.1 broadcast_add_fusion
  5.0 0.1 copy.31
  5.1 0.4 fusion.44
  5.5 4.3 scatter_custom_fusion
  9.9 1.9 concatenate.7
  11.8 11.8 %gather_fusion.1 = bf16[1152,2048]{1,0:T(8,128)(2,1)} fusion(bf16[129,2048]{1,0:T(8,128)(2,1)} %concatenate.7, s32[2048]{0:T(1024)S(1)} %get-tuple-element.8), kind=kCustom, calls=%fused_computation.1 | custom fusion | bytes 9441792 | tf_op jit(solution)/shard_map/gather | solution.py:30
  23.5 8.1 %reshape.122 = bf16[128,1,9,2048]{3,2,0,1:T(8,128)(2,1)} reshape(bf16[1152,2048]{1,0:T(8,128)(2,1)} %gather_fusion.1) | data formatting | bytes 9437184 | tf_op jit(solution)/shard_map/reshape | solution.py:30
  31.7 0.0 copy-start.3
  31.7 11.2 %all-to-all-start.1 = ((bf16[128,1,9,2048]{3,2,1,0:T(8,128)(2,1)}), bf16[128,1,9,2048]{3,2,1,0:T(8,128)(2,1)}, u32[]{:S(2)}, u32[]{:S(2)}) async-start(bf16[128,1,9,2048]{3,2,1,0:T(8,128)(2,1)} %bitcast.149), calls=%async_computation.1 | async-start | bytes 16777216 | tf_op jit(solution)/shard_map/all_to_all | solution.py:33
  42.8 0.0 copy-done.3
  42.8 0.1 copy.26
  42.9 0.1 reshape.131
  43.0 1.1 convert_element_type.56
  44.2 0.9 fusion
  45.1 2.4 concatenate.6
  47.5 13.4 %gather_fusion = bf16[1152,2048]{1,0:T(8,128)(2,1)} fusion(bf16[1025,2048]{1,0:T(8,128)(2,1)} %concatenate.6, s32[2048]{0:T(1024)S(1)} %get-tuple-element.9), kind=kCustom, calls=%fused_computation | custom fusion | bytes 9441792 | tf_op jit(solution)/shard_map/gather | solution.py:31
  60.9 8.0 %reshape.119 = bf16[128,1,9,2048]{3,2,0,1:T(8,128)(2,1)} reshape(bf16[1152,2048]{1,0:T(8,128)(2,1)} %gather_fusion) | data formatting | bytes 9437184 | tf_op jit(solution)/shard_map/reshape | solution.py:31
  68.9 78.4 %all-to-all-done.1 = bf16[128,1,9,2048]{3,2,1,0:T(8,128)(2,1)} async-done(((bf16[128,1,9,2048]{3,2,1,0:T(8,128)(2,1)}), bf16[128,1,9,2048]{3,2,1,0:T(8,128)(2,1)}, u32[]{:S(2)}, u32[]{:S(2)}) %all-to-all-start.1) | async-done | bytes 4718624 | tf_op jit(solution)/shard_map/all_to_all | solution.py:33
  147.2 6.9 %all-to-all-start = ((bf16[128,1,9,2048]{3,2,1,0:T(8,128)(2,1)}), bf16[128,1,9,2048]{3,2,1,0:T(8,128)(2,1)}, u32[]{:S(2)}, u32[]{:S(2)}) async-start(bf16[128,1,9,2048]{3,2,1,0:T(8,128)(2,1)} %bitcast.150), calls=%async_computation | async-start | bytes 16777216 | tf_op jit(solution)/shard_map/all_to_all | solution.py:34
  154.2 0.0 copy-done
  154.2 0.0 copy-start.4
  154.2 13.7 %fusion.2 = f32[128,9,768]{2,0,1:T(8,128)} fusion(bf16[1,2048,768]{2,1,0:T(8,128)(2,1)S(1)} %copy-done, bf16[128,1,9,2048]{3,2,1,0:T(8,128)(2,1)} %all-to-all-done.1), kind=kOutput, calls=%fused_computation.11 | convolution fusion | flops 3623878656 | bytes 11403264 | tf_op jit(solution)/shard_map/secd,edf->secf/dot_general | solution.py:36
  167.9 0.0 copy-done.4
  167.9 14.0 %fusion.4 = f32[128,9,768]{2,0,1:T(8,128)} fusion(bf16[1,2048,768]{2,1,0:T(8,128)(2,1)S(1)} %copy-done.4, bf16[128,1,9,2048]{3,2,1,0:T(8,128)(2,1)} %all-to-all-done.1), kind=kOutput, calls=%fused_computation.13 | convolution fusion | flops 3623878656 | bytes 11403264 | tf_op jit(solution)/shard_map/secd,edf->secf/dot_general | solution.py:39
  181.9 77.0 %all-to-all-done = bf16[128,1,9,2048]{3,2,1,0:T(8,128)(2,1)} async-done(((bf16[128,1,9,2048]{3,2,1,0:T(8,128)(2,1)}), bf16[128,1,9,2048]{3,2,1,0:T(8,128)(2,1)}, u32[]{:S(2)}, u32[]{:S(2)}) %all-to-all-start) | async-done | bytes 4718624 | tf_op jit(solution)/shard_map/all_to_all | solution.py:34
  258.9 15.6 %fusion.38 = (bf16[128,9,768]{2,0,1:T(8,128)(2,1)S(1)}, bf16[128,1,9,768]{3,0,2,1:T(8,128)(2,1)S(1)}) fusion(f32[128,9,768]{2,0,1:T(8,128)} %fusion.2, f32[128,9,768]{2,0,1:T(8,128)} %fusion.4, bf16[1,768,2048]{2,1,0:T(8,128)(2,1)} %param.13, bf16[128,1,9,2048]{3,2,1,0:T(8,128)(2,1)} %all-to-all-done), kind=kOutput, calls=%fused_computation.50 | convolution fusion | flops 3635380224 | bytes 18481152 | tf_op jit(solution)/shard_map/secd,efd->secf/dot_general | solution.py:43
  274.6 0.0 copy-start.10
  274.6 0.0 copy-start.6
  274.6 0.0 copy-start.5
  274.6 6.2 %fusion.21 = f32[128,9,2048]{2,0,1:T(8,128)} fusion(bf16[1,2048,768]{2,1,0:T(8,128)(2,1)S(1)} %copy-done, bf16[128,1,9,768]{3,0,2,1:T(8,128)(2,1)S(1)} %get-tuple-element.5), kind=kOutput, calls=%fused_computation.35 | convolution fusion | flops 3623878656 | bytes 14352384 | tf_op jit(solution)/shard_map/secf,edf->secd/dot_general | solution.py:51
  280.8 0.0 copy-done.10
  280.8 0.0 copy-done.6
  280.8 0.0 copy-done.5
  280.8 6.7 %fusion.1 = bf16[128,1,9,2048]{3,0,2,1:T(8,128)(2,1)S(1)} fusion(f32[128,9,2048]{2,0,1:T(8,128)} %fusion.21, bf16[128,9,768]{2,0,1:T(8,128)(2,1)S(1)} %get-tuple-element.4, bf16[1,2048,768]{2,1,0:T(8,128)(2,1)S(1)} %copy-done.5), kind=kOutput, calls=%fused_computation.10 | convolution fusion | flops 3628597248 | bytes 19070976 | tf_op jit(solution)/shard_map/secf,edf->secd/dot_general | solution.py:52
  287.6 6.4 %copy.36 = bf16[128,1,9,2048]{3,2,1,0:T(8,128)(2,1)} copy(bf16[128,1,9,2048]{3,0,2,1:T(8,128)(2,1)S(1)} %fusion.1) | data formatting | bytes 9437184 | tf_op jit(solution)/shard_map/convert_element_type | solution.py:53
  294.0 0.0 copy-start.7
  294.0 7.8 %all-to-all-start.2 = ((bf16[128,1,9,2048]{3,2,1,0:T(8,128)(2,1)}), bf16[128,1,9,2048]{3,2,1,0:T(8,128)(2,1)}, u32[]{:S(2)}, u32[]{:S(2)}) async-start(bf16[128,1,9,2048]{3,2,1,0:T(8,128)(2,1)} %copy.36), calls=%async_computation.2 | async-start | bytes 16777216 | tf_op jit(solution)/shard_map/all_to_all | solution.py:54
  301.7 0.0 copy-done.7
  301.7 0.0 copy-start.11
  301.8 22.3 %fusion.28 = bf16[1,2048,768]{2,1,0:T(8,128)(2,1)} fusion(bf16[128,9,768]{2,0,1:T(8,128)(2,1)S(1)} %copy-done.7, bf16[128,9,2048]{2,1,0:T(8,128)(2,1)} %bitcast.35), kind=kOutput, calls=%fused_computation.42 | convolution fusion | flops 3625451520 | bytes 9633792 | tf_op jit(solution)/shard_map/secd,secf->edf/dot_general | solution.py:61
  324.0 0.0 copy-done.11
  324.0 0.0 copy-start.8
  324.0 0.0 copy-start.9
  324.0 22.3 %fusion.27 = bf16[1,2048,768]{2,1,0:T(8,128)(2,1)} fusion(bf16[128,9,2048]{2,1,0:T(8,128)(2,1)} %bitcast.35, bf16[128,1,9,768]{3,0,2,1:T(8,128)(2,1)S(1)} %copy-done.11), kind=kOutput, calls=%fused_computation.41 | convolution fusion | flops 3625451520 | bytes 9633792 | tf_op jit(solution)/shard_map/secd,secf->edf/dot_general | solution.py:58
  346.4 0.0 copy-done.8
  346.4 0.0 copy-done.9
  346.4 17.8 %fusion.29 = bf16[1,768,2048]{2,1,0:T(8,128)(2,1)} fusion(bf16[128,1,9,2048]{3,2,1,0:T(8,128)(2,1)} %all-to-all-done, f32[128,9,768]{2,0,1:T(8,128)S(1)} %copy-done.9, f32[128,9,768]{2,0,1:T(8,128)S(1)} %copy-done.8), kind=kOutput, calls=%fused_computation.43 | convolution fusion | flops 3630759936 | bytes 14942208 | tf_op jit(solution)/shard_map/secf,secd->efd/dot_general | solution.py:55
  364.2 41.9 %all-to-all-done.2 = bf16[128,1,9,2048]{3,2,1,0:T(8,128)(2,1)} async-done(((bf16[128,1,9,2048]{3,2,1,0:T(8,128)(2,1)}), bf16[128,1,9,2048]{3,2,1,0:T(8,128)(2,1)}, u32[]{:S(2)}, u32[]{:S(2)}) %all-to-all-start.2) | async-done | bytes 4718624 | tf_op jit(solution)/shard_map/all_to_all | solution.py:54
  406.1 8.5 %reshape.128 = bf16[1152,2048]{1,0:T(8,128)(2,1)} reshape(bf16[128,1,9,2048]{3,2,1,0:T(8,128)(2,1)} %all-to-all-done.2) | data formatting | bytes 9437184 | tf_op jit(solution)/shard_map/reshape | solution.py:64
  414.7 0.0 copy-start.1
  414.7 11.9 %gather_fusion.2 = bf16[1024,2048]{1,0:T(8,128)(2,1)} fusion(bf16[1152,2048]{1,0:T(8,128)(2,1)} %reshape.128, s32[1024]{0:T(1024)S(1)} %broadcast_clamp_fusion), kind=kCustom, calls=%fused_computation.2 | custom fusion | bytes 8392704 | tf_op jit(solution)/shard_map/gather | solution.py:65
  426.6 5.9 %bitcast_reduce_fusion = bf16[128,2048]{1,0:T(8,128)(2,1)} fusion(bf16[1024,2048]{1,0:T(8,128)(2,1)} %gather_fusion.2), kind=kLoop, calls=%fused_computation.19 | loop fusion | flops 1835008 | bytes 4718592 | tf_op jit(solution)/shard_map/reduce_sum | solution.py:66
  432.5 0.0 copy-done.1
  (8 shorter events, 0.1 us)
Async XLA Ops:
  0.6 153.5 %copy-start = (bf16[1,2048,768]{2,1,0:T(8,128)(2,1)S(1)}, bf16[1,2048,768]{2,1,0:T(8,128)(2,1)}, u32[]{:S(2)}) copy-start(bf16[1,2048,768]{2,1,0:T(8,128)(2,1)} %param.11) | copy-start | bytes 9437188
  3.1 0.8 copy-start.2
  31.7 11.2 %copy-start.3 = (bf16[128,8]{0,1:T(8,128)(2,1)S(1)}, bf16[128,8]{0,1:T(8,128)(2,1)}, u32[]{:S(2)}) copy-start(bf16[128,8]{0,1:T(8,128)(2,1)} %param.10) | copy-start | bytes 6148
  31.7 115.6 %all-to-all-start.1 = ((bf16[128,1,9,2048]{3,2,1,0:T(8,128)(2,1)}), bf16[128,1,9,2048]{3,2,1,0:T(8,128)(2,1)}, u32[]{:S(2)}, u32[]{:S(2)}) async-start(bf16[128,1,9,2048]{3,2,1,0:T(8,128)(2,1)} %bitcast.149), calls=%async_computation.1 | async-start | bytes 16777216 | tf_op jit(solution)/shard_map/all_to_all | solution.py:33
  147.2 111.7 %all-to-all-start = ((bf16[128,1,9,2048]{3,2,1,0:T(8,128)(2,1)}), bf16[128,1,9,2048]{3,2,1,0:T(8,128)(2,1)}, u32[]{:S(2)}, u32[]{:S(2)}) async-start(bf16[128,1,9,2048]{3,2,1,0:T(8,128)(2,1)} %bitcast.150), calls=%async_computation | async-start | bytes 16777216 | tf_op jit(solution)/shard_map/all_to_all | solution.py:34
  154.2 13.7 %copy-start.4 = (bf16[1,2048,768]{2,1,0:T(8,128)(2,1)S(1)}, bf16[1,2048,768]{2,1,0:T(8,128)(2,1)}, u32[]{:S(2)}) copy-start(bf16[1,2048,768]{2,1,0:T(8,128)(2,1)} %param.12) | copy-start | bytes 9437188
  274.6 6.3 %copy-start.10 = (bf16[128,1,9,768]{3,0,2,1:T(8,128)(2,1)}, bf16[128,1,9,768]{3,0,2,1:T(8,128)(2,1)S(1)}, u32[]{:S(2)}) copy-start(bf16[128,1,9,768]{3,0,2,1:T(8,128)(2,1)S(1)} %get-tuple-element.5) | copy-start | bytes 5308420
  274.6 6.3 %copy-start.6 = (bf16[128,9,768]{2,0,1:T(8,128)(2,1)}, bf16[128,9,768]{2,0,1:T(8,128)(2,1)S(1)}, u32[]{:S(2)}) copy-start(bf16[128,9,768]{2,0,1:T(8,128)(2,1)S(1)} %get-tuple-element.4) | copy-start | bytes 5308420
  274.6 6.3 %copy-start.5 = (bf16[1,2048,768]{2,1,0:T(8,128)(2,1)S(1)}, bf16[1,2048,768]{2,1,0:T(8,128)(2,1)}, u32[]{:S(2)}) copy-start(bf16[1,2048,768]{2,1,0:T(8,128)(2,1)} %param.12) | copy-start | bytes 9437188
  294.0 7.8 %copy-start.7 = (bf16[128,9,768]{2,0,1:T(8,128)(2,1)S(1)}, bf16[128,9,768]{2,0,1:T(8,128)(2,1)}, u32[]{:S(2)}) copy-start(bf16[128,9,768]{2,0,1:T(8,128)(2,1)} %copy-done.6) | copy-start | bytes 5308420
  294.0 112.2 %all-to-all-start.2 = ((bf16[128,1,9,2048]{3,2,1,0:T(8,128)(2,1)}), bf16[128,1,9,2048]{3,2,1,0:T(8,128)(2,1)}, u32[]{:S(2)}, u32[]{:S(2)}) async-start(bf16[128,1,9,2048]{3,2,1,0:T(8,128)(2,1)} %copy.36), calls=%async_computation.2 | async-start | bytes 16777216 | tf_op jit(solution)/shard_map/all_to_all | solution.py:54
  301.7 22.3 %copy-start.11 = (bf16[128,1,9,768]{3,0,2,1:T(8,128)(2,1)S(1)}, bf16[128,1,9,768]{3,0,2,1:T(8,128)(2,1)}, u32[]{:S(2)}) copy-start(bf16[128,1,9,768]{3,0,2,1:T(8,128)(2,1)} %copy-done.10) | copy-start | bytes 5308420
  324.0 22.3 %copy-start.8 = (f32[128,9,768]{2,0,1:T(8,128)S(1)}, f32[128,9,768]{2,0,1:T(8,128)}, u32[]{:S(2)}) copy-start(f32[128,9,768]{2,0,1:T(8,128)} %fusion.2) | copy-start | bytes 10616836
  324.0 22.3 %copy-start.9 = (f32[128,9,768]{2,0,1:T(8,128)S(1)}, f32[128,9,768]{2,0,1:T(8,128)}, u32[]{:S(2)}) copy-start(f32[128,9,768]{2,0,1:T(8,128)} %fusion.4) | copy-start | bytes 10616836
  414.7 17.8 %copy-start.1 = (bf16[1,2048,768]{2,1,0:T(8,128)(2,1)S(1)}, bf16[1,2048,768]{2,1,0:T(8,128)(2,1)}, u32[]{:S(2)}) copy-start(bf16[1,2048,768]{2,1,0:T(8,128)(2,1)} %param.11) | copy-start | bytes 9437188
where the time goes:
time: 441 us; the launch traced here: 433 us
  waiting for transfers between devices  197 us (45%)
  matrix products  119 us (27%)
  local copies, waits for them, and re-layouts  79.3 us (18%)
  starting transfers between devices  25.8 us (6%)
  other arithmetic  10.5 us (2%)
    all_to_all x1, waiting for transfers between devices, body(): lax.all_to_all(sent_rows, ('node', 'local'), split_axis=0, concat_axis=0,...  78.4 us
    all_to_all x1, waiting for transfers between devices, body(): lax.all_to_all(sent_grad, ('node', 'local'), split_axis=0, concat_axis=0,...  77 us
    all_to_all x1, waiting for transfers between devices, body(): lax.all_to_all(slot_grad, ('node', 'local'), split_axis=0, concat_axis=0,...  41.9 us
    dot_general x1, matrix products, body(): jnp.einsum('secd,secf->edf', got_rows, gate_grad, preferred_element_type=...  22.3 us
    dot_general x1, matrix products, body(): jnp.einsum('secd,secf->edf', got_rows, up_grad, preferred_element_type=jn...  22.3 us
    dot_general x1, matrix products, body(): jnp.einsum('secf,secd->efd', hidden, got_grad, preferred_element_type=jnp...  17.8 us
    dot_general x1, matrix products, body(): jnp.einsum('secd,efd->secf', got_grad, down_weight, preferred_element_typ...  15.6 us
    dot_general x1, matrix products, body(): jnp.einsum('secd,edf->secf', got_rows, up_weight, preferred_element_type=...  14 us
  transfers between devices with their start and end apart: 3, of which 3 were waited for; matrix products, arithmetic and copies ran while one was open for 27% of the time, Pallas kernels for 0%

commit v1 on v0

v1 whole, which is shorter than its diff:
```python
import functools

import jax
import jax.numpy as jnp
from jax import lax
from jax.experimental import pallas as pl
from jax.experimental.pallas import tpu as pltpu
from jax.sharding import PartitionSpec as P

MESH = pl.DeviceIdType.MESH
BF, F32 = jnp.bfloat16, jnp.float32
D, FF, TOK, TOP, SLOTS = 2048, 768, 128, 8, 9
WIDTH = (640, 768, 640)
START = (0, 640, 1408)
HALF = 384
ROWS = 1152
MAIN_A, TAILS = 512, 128


def place():
    node, local = lax.axis_index("node"), lax.axis_index("local")
    return local // 2, (node % 8) // 2, (node // 8) * 2 + local % 2, node % 2


def order(j, x, y, z):
    return ((x, y, z), (y, z, x), (z, x, y))[j]


def device(j, a, b, c, core):
    x, y, z = ((a, b, c), (c, a, b), (b, c, a))[j]
    return ((z // 2) * 8 + y * 2 + core, x * 2 + z % 2)


def canon(j, ref, lead, par, b, c, cols):
    q = (par + b + c) % 2
    every = slice(None)
    if j == 0:
        at = (par, c // 2, c % 2, b // 2, b % 2, every)
    elif j == 1:
        at = (par, b // 2, b % 2, every, q, c // 2)
    else:
        at = (par, every, q, c // 2, c % 2, b // 2)
    return ref.at[lead + at + (every, cols)]


def remote(src, dst, ssem, rsem, dev):
    return pltpu.make_async_remote_copy(
        src_ref=src, dst_ref=dst, send_sem=ssem, recv_sem=rsem, device_id=dev, device_id_type=MESH
    )


def greet(partners):
    barrier = pltpu.get_barrier_semaphore()
    for dev in partners:
        pl.semaphore_signal(barrier, inc=1, device_id=dev, device_id_type=MESH)
    pl.semaphore_wait(barrier, len(partners))


def partners_of(x, y, z, core):
    out = [device(0, x, y, z, 1 - core)]
    for d in (1, 2, 3):
        out.append(device(0, (x + d) % 4, y, z, core))
        out.append(device(0, x, (y + d) % 4, z, core))
        out.append(device(0, x, y, (z + d) % 4, core))
    return out


def iota(shape, dim):
    return lax.broadcasted_iota(jnp.int32, shape, dim)


def tail_perm(j, array):
    row, col = iota((128, 256), 0), iota((128, 256), 1)
    core, x, y, z = row % 2, (row // 2) % 4, (row // 8) % 4, row // 32
    a, b, c = order(j, x, y, z)
    want = c * 64 + b * 16 + array * 8 + a * 2 + core
    return (col == want).astype(F32).astype(BF)


def tail_spread(j, half):
    row, col = iota((256, 128), 0), iota((256, 128), 1)
    c, b, h, a, core = row // 64, (row // 16) % 4, (row // 8) % 2, (row // 2) % 4, row % 2
    x, y, z = ((a, b, c), (c, a, b), (b, c, a))[j]
    return ((col == z * 32 + y * 8 + x * 2 + core) & (h == half)).astype(F32).astype(BF)


def over_rows(left, right):
    return lax.dot_general(left, right, (((0,), (0,)), ((), ())), preferred_element_type=F32)


def across(left, right):
    return lax.dot_general(left, right, (((1,), (1,)), ((), ())), preferred_element_type=F32)


def tile(i):
    return pl.ds(pl.multiple_of(i * 256, 256), 256)


def kernel(tok, grad, meta, gate_w, up_w, down_w, out, gate_out, up_out, down_out, *rest):
    (R, RT, R1, RT1), scr = (rest[3 * i : 3 * i + 3] for i in range(4)), rest[12:]
    T, S, ST, FT, ST2, R2, RT2, KEEP, OWN = (scr[3 * i : 3 * i + 3] for i in range(9))
    XG, XT, SG, SGT, WG, WU, WD, HID, GG, UG, metas, pos = scr[27:39]
    (ag_s, ag_r, sib_s, sib_r, mag_s, mag_r, msib_s, msib_r, loc, locm,
     p2_s, p2_r, p2t_s, p2t_r, p3_s, p3_r, p3t_s, p3t_r, locp, loct,
     r1_s, r1_r, r1t_s, r1t_r, r2_s, r2_r, r2t_s, r2t_r, l2, l2t,
     ps_s, ps_r, q_s, q_r, wsem, osem, done) = scr[39:]
    x, y, z, core = place()
    axes = [order(j, x, y, z) for j in range(3)]
    sib = device(0, x, y, z, 1 - core)
    weights = ((gate_w, WG), (up_w, WU), (down_w, WD))
    for i, (src, dst) in enumerate(weights):
        pltpu.make_async_copy(src.at[0], dst, wsem.at[i]).start()
    greet(partners_of(x, y, z, core))
    ins = (tok, grad)
    sends, early = [], []

    def go(cp, kept=sends):
        cp.start()
        kept.append(cp)

    def got(ref, rsem):
        remote(ref, ref, ag_s.at[0, 0, 0], rsem, sib).wait_recv()

    def landed(ref, sem):
        pltpu.make_async_copy(ref, ref, sem).wait()

    def cols_of(j):
        return pl.ds(START[j], WIDTH[j])

    for j in range(3):
        a, b, c = axes[j]
        for d in (2, 1, 3):
            dev = device(j, (a + d) % 4, b, c, core)
            go(remote(meta, metas.at[j, a, core], mag_s.at[j, d], mag_r.at[j, a], dev))
    for d in (2, 1, 3):
        for j in range(3):
            a, b, c = axes[j]
            dev = device(j, (a + d) % 4, b, c, core)
            for r in range(2):
                src = ins[r].at[:, cols_of(j)]
                go(remote(src, T[j].at[r, a, core], ag_s.at[j, d, r], ag_r.at[j, a, r], dev))
    for j in range(3):
        a, b, c = axes[j]
        go(remote(meta, metas.at[j, a, core], msib_s.at[j, a], msib_r.at[j, a], sib))
        pltpu.make_async_copy(meta, metas.at[j, a, core], locm.at[j]).start()
        for r in range(2):
            src = ins[r].at[:, cols_of(j)]
            go(remote(src, T[j].at[r, a, core], sib_s.at[j, a, r], sib_r.at[j, a, r], sib))
            pltpu.make_async_copy(src, T[j].at[r, a, core], loc.at[j, r]).start()

    for d in (1, 3, 2):
        for j in range(3):
            s = (axes[j][0] + d) % 4
            m = metas.at[j, s, core]
            got(m, mag_r.at[j, s])
            go(remote(m, m, msib_s.at[j, s], msib_r.at[j, s], sib))
        for j in range(3):
            s = (axes[j][0] + d) % 4
            for r in range(2):
                t = T[j].at[r, s, core]
                got(t, ag_r.at[j, s, r])
                go(remote(t, t, sib_s.at[j, s, r], sib_r.at[j, s, r], sib), early)

    before = (iota((TOK, TOK), 0) < iota((TOK, TOK), 1)).astype(F32).astype(BF)

    def one_hot(j, s, gate, last):
        a = axes[j][0]
        e = iota((16, 1), 0)
        dev = device(j, a, e // 4, e % 4, core)
        expert = (dev[0] * 8 + dev[1]).astype(F32)
        parts = []
        for k in range(2):
            info = metas[j, s, k]
            value = jnp.ones((16, TOK), F32)
            if gate:
                value = jnp.zeros((16, TOK), F32)
                for i in range(TOP):
                    hit = info[i : i + 1, :] == expert
                    value = value + jnp.where(hit, info[TOP + i : TOP + i + 1, :], 0.0)
            at = pos[j, s, k][:, None, :]
            if last:
                hit = (at == 8.0) & (iota((16, 8, TOK), 1) == 2 * s + k)
            else:
                hit = at * 2.0 + k == iota((16, 16, TOK), 1).astype(F32)
            parts.append(jnp.where(hit, value[:, None, :], 0.0).reshape(128 if last else 256, TOK))
        return jnp.concatenate(parts, axis=1).astype(BF)

    def find_slots(j):
        a = axes[j][0]
        e = iota((16, 1), 0)
        dev = device(j, a, e // 4, e % 4, core)
        expert = (dev[0] * 8 + dev[1]).astype(F32)
        for s in range(4):
            for k in range(2):
                info = metas[j, s, k]
                named = jnp.zeros((16, TOK), F32)
                for i in range(TOP):
                    named = named + jnp.where(info[i : i + 1, :] == expert, 1.0, 0.0)
                earlier = jnp.dot(named.astype(BF), before, preferred_element_type=F32)
                pos[j, s, k] = jnp.where(named > 0.5, earlier, -1.0)

    def gather(j, par):
        a, b, c = axes[j]
        w = WIDTH[j]
        for h in range(2):
            s = 2 * h + (par + b + c) % 2
            for r in range(2):
                rows = T[j][r, s].reshape(2 * TOK, w)
                main = jnp.dot(one_hot(j, s, r == 1, False), rows, preferred_element_type=F32)
                S[j][:, :, r, par, h] = main.astype(BF).reshape(4, 4, 16, w)

    def gather_tails(j):
        w = WIDTH[j]
        tails = []
        for r in range(2):
            rows = jnp.zeros((TAILS, w), F32)
            for s in range(4):
                picked = T[j][r, s].reshape(2 * TOK, w)
                rows = rows + jnp.dot(one_hot(j, s, r == 1, True), picked, preferred_element_type=F32)
            tails.append(rows.reshape(16, 8, w))
        ST[j][...] = jnp.concatenate(tails, axis=1).astype(BF).reshape(4, 4, 16, w)

    def along_b(j, par):
        a, b, c = axes[j]
        for d in (2, 1, 3):
            t = (b + d) % 4
            dev = device(j, a, t, c, core)
            go(remote(S[j].at[t, :, :, par], R[j].at[b, :, :, par], p2_s.at[j, par, d], p2_r.at[j, par, b], dev))
            if par == 0:
                go(remote(ST[j].at[t], RT[j].at[b], p2t_s.at[j, d], p2t_r.at[j, b], dev))

    def along_c(j, par, d, main, tail):
        a, b, c = axes[j]
        s = (b + d) % 4
        dst = canon(j, XG, (slice(None),), par, s, c, cols_of(j))
        for dc in (2, 1, 3):
            t = (c + dc) % 4
            dev = device(j, a, b, t, core)
            go(remote(main.at[s, t, :, par], dst, p3_s.at[j, par, d, dc], p3_r.at[j, par, c, s], dev))
            if par == 0:
                go(remote(tail.at[s, t], FT[j].at[c, s], p3t_s.at[j, d, dc], p3t_r.at[j, c, s], dev))
        pltpu.make_async_copy(main.at[s, c, :, par], dst, locp.at[j, par, d]).start()
        if par == 0:
            pltpu.make_async_copy(tail.at[s, c], FT[j].at[c, s], loct.at[j, d]).start()

    def pass_on(par):
        for d in (1, 3, 2):
            for j in range(3):
                s = (axes[j][1] + d) % 4
                got(R[j].at[s, :, :, par], p2_r.at[j, par, s])
                if par == 0:
                    got(RT[j].at[s], p2t_r.at[j, s])
                along_c(j, par, d, R[j], RT[j])

    def arrive(par, offsets):
        for j in range(3):
            a, b, c = axes[j]
            for db in offsets:
                s = (b + db) % 4
                f = canon(j, XG, (slice(None),), par, s, c, cols_of(j))
                landed(f, locp.at[j, par, db])
                if par == 0:
                    landed(FT[j].at[c, s], loct.at[j, db])
                for dc in (1, 2, 3):
                    t = (c + dc) % 4
                    f = canon(j, XG, (slice(None),), par, s, t, cols_of(j))
                    got(f, p3_r.at[j, par, t, s])
                    if par == 0:
                        got(FT[j].at[t, s], p3t_r.at[j, t, s])

    first, size = (0, MAIN_A + TAILS), (MAIN_A + TAILS, MAIN_A)

    def rows_of(r, par):
        main = XG[r, par].reshape(MAIN_A, D)
        return jnp.concatenate([main, XT[r]], axis=0) if par == 0 else main

    def forward(par):
        span = pl.ds(first[par], size[par])

        def hidden_tile(i, carry):
            cols = tile(i)
            rows = rows_of(0, par)
            gate_pre = jnp.dot(rows, WG[:, cols], preferred_element_type=F32)
            up_pre = jnp.dot(rows, WU[:, cols], preferred_element_type=F32)
            hidden_grad = across(rows_of(1, par), WD[cols, :])
            logistic = jax.nn.sigmoid(gate_pre)
            silu_gate = gate_pre * logistic
            HID[span, cols] = (silu_gate * up_pre).astype(BF)
            UG[span, cols] = (hidden_grad * silu_gate).astype(BF)
            GG[span, cols] = (hidden_grad * up_pre * logistic * (1.0 + gate_pre * (1.0 - logistic))).astype(BF)
            return carry

        lax.fori_loop(0, FF // 256, hidden_tile, 0)

        def slot_tile(i, carry):
            cols = tile(i)
            rows = (across(GG[span, :], WG[cols, :]) + across(UG[span, :], WU[cols, :])).astype(BF)
            SG[par, :, :, :, :, :, :, cols] = rows[:MAIN_A].reshape(2, 2, 2, 2, 2, 16, 256)
            if par == 0:
                SGT[:, cols] = rows[MAIN_A:]
            return carry

        lax.fori_loop(0, D // 256, slot_tile, 0)

    def in_tile(i, carry):
        cols = tile(i)
        parts = [XG[0, 0, :, :, :, :, :, :, cols].reshape(MAIN_A, 256), XT[0, :, cols]]
        rows = jnp.concatenate(parts + [XG[0, 1, :, :, :, :, :, :, cols].reshape(MAIN_A, 256)], axis=0)
        WG[cols, :] = over_rows(rows, GG[...]).astype(BF)
        WU[cols, :] = over_rows(rows, UG[...]).astype(BF)
        return carry

    def down_tile(i, carry):
        cols = tile(i)
        rows = jnp.concatenate([rows_of(1, 0), rows_of(1, 1)], axis=0)
        WD[cols, :] = over_rows(HID[:, cols], rows).astype(BF)
        return carry

    def back_c(par):
        for d in (2, 1, 3):
            for j in range(3):
                a, b, c = axes[j]
                t = (c + d) % 4
                dev = device(j, a, b, t, core)
                for bl in range(2):
                    if j == 0:
                        at = (par, t // 2, t % 2, slice(None), bl, slice(None))
                    elif j == 1:
                        at = (par, slice(None), bl, slice(None), (par + bl + t) % 2, t // 2)
                    else:
                        at = (par, slice(None), (par + bl + t) % 2, t // 2, t % 2, slice(None))
                    src = SG.at[at + (slice(None), cols_of(j))]
                    go(remote(src, R1[j].at[c, par, bl], r1_s.at[j, par, d, bl], r1_r.at[j, par, c, bl], dev))
        if par == 0:
            for j in range(3):
                a, b, c = axes[j]
                lo, hi = START[j], START[j] + WIDTH[j] - HALF
                rows = jnp.dot(tail_spread(j, 0), SGT[:, lo : lo + HALF], preferred_element_type=F32)
                rows = rows + jnp.dot(tail_spread(j, 1), SGT[:, hi : hi + HALF], preferred_element_type=F32)
                ST2[j][...] = rows.astype(BF).reshape(4, 4, 16, HALF)
                for d in (2, 1, 3):
                    t = (c + d) % 4
                    dev = device(j, a, b, t, core)
                    go(remote(ST2[j].at[t], RT1[j].at[c], r1t_s.at[j, d], r1t_r.at[j, c], dev))
        for j in range(3):
            c = axes[j][2]
            back_b(j, par, 0, lambda t: canon(j, SG, (), par, t, c, cols_of(j)), ST2[j].at[c])

    def back_b(j, par, d, main, tail):
        a, b, c = axes[j]
        s = (c + d) % 4
        for db in (2, 1, 3):
            t = (b + db) % 4
            dev = device(j, a, t, c, core)
            go(remote(main(t), R2[j].at[b, s, par], r2_s.at[j, par, d, db], r2_r.at[j, par, b, s], dev))
            if par == 0:
                go(remote(tail.at[t], RT2[j].at[b, s], r2t_s.at[j, d, db], r2t_r.at[j, b, s], dev))
        pltpu.make_async_copy(main(b), R2[j].at[b, s, par], l2.at[j, par, d]).start()
        if par == 0:
            pltpu.make_async_copy(tail.at[b], RT2[j].at[b, s], l2t.at[j, d]).start()

    def pass_back(par):
        for d in (1, 3, 2):
            for j in range(3):
                s = (axes[j][2] + d) % 4
                for bl in range(2):
                    got(R1[j].at[s, par, bl], r1_r.at[j, par, s, bl])
                if par == 0:
                    got(RT1[j].at[s], r1t_r.at[j, s])

                def main(t, j=j, s=s):
                    if j == 2:
                        return R1[j].at[s, par, t % 2, :, t // 2]
                    return R1[j].at[s, par, t % 2, t // 2]

                back_b(j, par, d, main, RT1[j].at[s])

    def returned(par):
        for j in range(3):
            a, b, c = axes[j]
            for dc in range(4):
                s = (c + dc) % 4
                landed(R2[j].at[b, s, par], l2.at[j, par, dc])
                if par == 0:
                    landed(RT2[j].at[b, s], l2t.at[j, dc])
                for db in (1, 2, 3):
                    t = (b + db) % 4
                    got(R2[j].at[t, s, par], r2_r.at[j, par, t, s])
                    if par == 0:
                        got(RT2[j].at[t, s], r2t_r.at[j, t, s])

    def combine(par):
        for j in range(3):
            a, b, c = axes[j]
            w = WIDTH[j]
            tails = RT2[j][...].reshape(256, HALF)
            for h in range(2):
                s = 2 * h + (par + b + c) % 2
                pick, low, high = [], [], []
                for k in range(2):
                    who = (core + k) % 2
                    at = pos[j, s, who][:, None, :]
                    row = iota((16, 16, TOK), 1)
                    hit = at * 2.0 + who.astype(F32) == row.astype(F32)
                    pick.append(jnp.where(hit, 1.0, 0.0).reshape(256, TOK))
                    hit = (at == 8.0) & (row == 2 * s + who)
                    low.append(jnp.where(hit, 1.0, 0.0).reshape(256, TOK))
                    hit = (at == 8.0) & (row == 8 + 2 * s + who)
                    high.append(jnp.where(hit, 1.0, 0.0).reshape(256, TOK))
                pick, low, high = (jnp.concatenate(p, axis=1).astype(BF) for p in (pick, low, high))
                total = over_rows(pick, R2[j][:, :, par, h].reshape(256, w))
                total = total + jnp.concatenate(
                    [over_rows(low, tails), over_rows(high, tails)[:, 2 * HALF - w :]], axis=1
                )
                i = 2 * par + h
                KEEP[j][h] = total[:TOK]
                T[j][0, i, 0] = total[TOK:].astype(BF)
                go(remote(T[j].at[0, i, 0], T[j].at[0, i, 1], ps_s.at[j, i], ps_r.at[j, i], sib))
        for j in range(3):
            a, b, c = axes[j]
            for h in range(2):
                s = 2 * h + (par + b + c) % 2
                i = 2 * par + h
                got(T[j].at[0, i, 1], ps_r.at[j, i])
                total = KEEP[j][h] + T[j][0, i, 1].astype(F32)

                @pl.when(s == a)
                def _():
                    OWN[j][...] = total

                @pl.when(s != a)
                def _():
                    T[j][1, i, 0] = total.astype(BF)
                    to_line(j, i, s).start()

    def to_line(j, i, s):
        a, b, c = axes[j]
        return remote(T[j].at[1, i, 0], T[j].at[1, a, 1], q_s.at[j, i], q_r.at[j, a], device(j, s, b, c, core))

    for j in range(3):
        a, b, c = axes[j]
        landed(metas.at[j, a, core], locm.at[j])
        for s in range(4):
            got(metas.at[j, s, 1 - core], msib_r.at[j, s])
        find_slots(j)
    for j in range(3):
        for r in range(2):
            landed(T[j].at[r, axes[j][0], core], loc.at[j, r])
            for s in range(4):
                got(T[j].at[r, s, 1 - core], sib_r.at[j, s, r])
        gather(j, 0)
        gather_tails(j)
        along_b(j, 0)
        along_c(j, 0, 0, S[j], ST[j])
    for j in range(3):
        gather(j, 1)
    for cp in early:
        cp.wait_send()
    pl.semaphore_signal(done, inc=1, device_id=sib, device_id_type=MESH)
    pass_on(0)
    arrive(0, (0,))
    for j in range(3):
        along_b(j, 1)
        along_c(j, 1, 0, S[j], ST[j])
    arrive(0, (1, 3, 2))
    for j in range(3):
        rows = FT[j][...].reshape(256, WIDTH[j])
        for r in range(2):
            XT[r, :, cols_of(j)] = jnp.dot(tail_perm(j, r), rows, preferred_element_type=F32).astype(BF)
    for i, (src, dst) in enumerate(weights):
        pltpu.make_async_copy(src.at[0], dst, wsem.at[i]).wait()
    forward(0)
    back_c(0)
    pass_on(1)
    pass_back(0)
    arrive(1, (0, 1, 3, 2))
    forward(1)
    back_c(1)
    pl.semaphore_wait(done, 1)
    returned(0)
    combine(0)
    lax.fori_loop(0, 4, in_tile, 0)
    pass_back(1)
    lax.fori_loop(4, 8, in_tile, 0)
    pltpu.make_async_copy(WG, gate_out.at[0], osem.at[0]).start()
    pltpu.make_async_copy(WU, up_out.at[0], osem.at[1]).start()
    lax.fori_loop(0, 3, down_tile, 0)
    pltpu.make_async_copy(WD, down_out.at[0], osem.at[2]).start()
    returned(1)
    combine(1)
    for j in range(3):
        a = axes[j][0]
        total = OWN[j][...]
        for d in (1, 3, 2):
            s = (a + d) % 4
            got(T[j].at[1, s, 1], q_r.at[j, s])
            total = total + T[j][1, s, 1].astype(F32)
        out[:, START[j] : START[j] + WIDTH[j]] = total.astype(BF)
    for cp in sends:
        cp.wait_send()
    for j in range(3):
        a, b, c = axes[j]
        for i in range(4):
            s = 2 * (i % 2) + (i // 2 + b + c) % 2

            @pl.when(s != a)
            def _():
                to_line(j, i, s).wait_send()

    for i, (src, dst) in enumerate(((WG, gate_out), (WU, up_out), (WD, down_out))):
        pltpu.make_async_copy(src, dst.at[0], osem.at[i]).wait()


def run(tokens, out_grad, meta, gate_weight, up_weight, down_weight):
    dma = pltpu.SemaphoreType.DMA
    vm = pltpu.VMEM
    any_spec = pl.BlockSpec(memory_space=pl.ANY)
    shape = jax.ShapeDtypeStruct
    scratch = [vm((2, 4, 2, TOK, w), BF) for w in WIDTH]
    scratch += [vm((4, 4, 2, 2, 2, 16, w), BF) for w in WIDTH]
    scratch += [vm((4, 4, 16, w), BF) for w in WIDTH] * 2
    scratch += [vm((4, 4, 16, HALF), BF)] * 3
    scratch += [vm((4, 4, 2, 2, 16, w), BF) for w in WIDTH]
    scratch += [vm((4, 4, 16, HALF), BF)] * 3
    scratch += [vm((2, TOK, w), F32) for w in WIDTH] + [vm((TOK, w), F32) for w in WIDTH]
    scratch += [vm((2, 2, 2, 2, 2, 2, 2, 16, D), BF), vm((2, TAILS, D), BF)]
    scratch += [vm((2, 2, 2, 2, 2, 2, 16, D), BF), vm((TAILS, D), BF)]
    scratch += [vm((D, FF), BF), vm((D, FF), BF), vm((FF, D), BF)] + [vm((ROWS, FF), BF)] * 3
    scratch += [vm((3, 4, 2, 16, TOK), F32)] * 2
    scratch += [dma((3, 4, 2))] * 4 + [dma((3, 4))] * 4 + [dma((3, 2)), dma((3,))]
    scratch += [dma((3, 2, 4))] * 2 + [dma((3, 4))] * 2 + [dma((3, 2, 4, 4))] * 2 + [dma((3, 4, 4))] * 2
    scratch += [dma((3, 2, 4)), dma((3, 4))]
    scratch += [dma((3, 2, 4, 2))] * 2 + [dma((3, 4))] * 2 + [dma((3, 2, 4, 4))] * 2 + [dma((3, 4, 4))] * 2
    scratch += [dma((3, 2, 4)), dma((3, 4))]
    scratch += [dma((3, 4))] * 4 + [dma((3,))] * 2 + [pltpu.SemaphoreType.REGULAR]
    outs = [shape((TOK, D), BF), shape((1, D, FF), BF), shape((1, D, FF), BF), shape((1, FF, D), BF)]
    outs += [shape((4, 4, 2, 2, 2, 16, w), BF) for w in WIDTH] + [shape((4, 4, 16, w), BF) for w in WIDTH]
    outs += [shape((4, 2, 2, 2, 2, 16, w), BF) for w in WIDTH] + [shape((4, 4, 16, HALF), BF)] * 3
    return pl.pallas_call(
        kernel,
        name="experts",
        out_shape=outs,
        in_specs=[any_spec] * 6,
        out_specs=[pl.BlockSpec(memory_space=pltpu.VMEM)] + [any_spec] * 15,
        scratch_shapes=scratch,
        compiler_params=pltpu.CompilerParams(collective_id=0, has_side_effects=True, vmem_limit_bytes=62 << 20),
    )(tokens, out_grad, meta, gate_weight, up_weight, down_weight)[:4]


def body(tokens, out_grad, expert_ids, gates, gate_weight, up_weight, down_weight):
    meta = jnp.concatenate([expert_ids.astype(F32), gates.astype(F32)], axis=1).T
    return tuple(run(tokens, out_grad, meta, gate_weight, up_weight, down_weight))


def solution(mesh):
    whole = ("node", "local")
    two, three = P(whole, None), P(whole, None, None)
    return jax.shard_map(
        body,
        mesh=mesh,
        in_specs=(two, two, two, two, three, three, three),
        out_specs=(two, three, three, three),
        check_vma=False,
    )
```

time: 441 us -> 191 us (0.43); the launches traced: 433 us -> 189 us
  waiting for transfers between devices: 197 us -> 0 us
  Pallas kernels: 0 us -> 176 us
  matrix products: 119 us -> 0 us
  local copies, waits for them, and re-layouts: 79.3 us -> 10.5 us
  starting transfers between devices: 25.8 us -> 0 us
  other arithmetic: 10.5 us -> 1.97 us
    all_to_all x3 -> x0, waiting for transfers between devices: 197 us -> none  [the longest x1 78.4 us: body(): lax.all_to_all(sent_rows, ('node', 'local'), split_axis=0, concat_axis=0,...]
    pallas_call x0 -> x1, Pallas kernels: none -> 176 us  [run(): pl.pallas_call(kernel, name='experts', out_shape=outs, in_specs=[any_spec...]
    dot_general x8 -> x0, matrix products: 119 us -> none  [the longest x1 22.3 us: body(): jnp.einsum('secd,secf->edf', got_rows, gate_grad, preferred_element_type=...]
    gather x3 -> x0, local copies, waits for them, and re-layouts: 37.1 us -> none  [the longest x1 13.4 us: body(): scaled_pad[owners].reshape(groups, exp_local, slot_cap, model_width)]
    all_to_all x3 -> x0, starting transfers between devices: 25.8 us -> none  [the longest x1 11.2 us: body(): lax.all_to_all(sent_rows, ('node', 'local'), split_axis=0, concat_axis=0,...]
    reshape x3 -> x0, local copies, waits for them, and re-layouts: 24.7 us -> none  [the longest x1 8.53 us: body(): back_rows = returned.reshape(experts * slot_cap, model_width)]
    unnamed x25 -> x8, local copies, waits for them, and re-layouts: 1.75 us -> 10.5 us
    convert_element_type x1 -> x0, local copies, waits for them, and re-layouts: 6.37 us -> none  [body(): slot_grad = (jnp.einsum('secf,edf->secd', gate_grad, gate_weight, preferr...]
  transfers between devices with their start and end apart: 3 -> 0, of which waited for: 3 -> 0; matrix products, arithmetic and copies ran while one was open for 27% -> 0% of each run, Pallas kernels for 0% -> 0%
where the time goes in v1:
time: 191 us; the launch traced here: 189 us
  Pallas kernels  176 us (92%)
  local copies, waits for them, and re-layouts  10.5 us (5%)
  other arithmetic  1.97 us (1%)
    pallas_call x1, Pallas kernels, run(): pl.pallas_call(kernel, name='experts', out_shape=outs, in_specs=[any_spec...  176 us
    unnamed x8, local copies, waits for them, and re-layouts  10.5 us

profile of v1, /device:TPU:13, one launch (start us, length us, event | category | flops | bytes accessed | tf_op | source)
XLA Modules:
  0.0 188.7 jit_solution(2207380004829982970)
XLA Ops:
  0.6 0.7 convert_element_type.6
  1.3 0.7 convert_element_type.7
  2.0 0.6 maximum_bitcast_fusion.meta
  2.6 175.6 %experts.1 = (bf16[128,2048]{1,0:T(8,128)(2,1)}, bf16[1,2048,768]{2,1,0:T(8,128)(2,1)}, bf16[1,2048,768]{2,1,0:T(8,128)(2,1)}, bf16[1,768,2048]{2,1,0:T(8,128)(2...) custom-call(bf16[128,2048]{1,0:T(8,128)(2,1)} %tok.1, ...), custom_call_target="tpu_custom_call" | custom-call | tf_op jit(solution)/shard_map/experts/pallas_call | solution.py:539
  178.2 1.9 copy.15
  180.1 0.0 copy-start.1
  180.1 3.9 %copy.16 = bf16[1,2048,768]{2,1,0:T(8,128)(2,1)} copy(bf16[1,2048,768]{2,1,0:T(8,128)(2,1)} %get-tuple-element.17) | data formatting | bytes 6291456
  184.0 0.0 copy-done.1
  184.0 0.0 copy-start
  184.0 1.7 copy.17
  185.7 1.4 copy-done
  187.1 1.7 copy.18
Async XLA Ops:
  180.1 3.9 %copy-start.1 = (bf16[1,2048,768]{2,1,0:T(8,128)(2,1)S(1)}, bf16[1,2048,768]{2,1,0:T(8,128)(2,1)}, u32[]{:S(2)}) copy-start(bf16[1,2048,768]{2,1,0:T(8,128)(2,1)} %get-tuple-element.18) | copy-start | bytes 9437188
  184.0 3.0 %copy-start = (bf16[1,768,2048]{2,1,0:T(8,128)(2,1)S(1)}, bf16[1,768,2048]{2,1,0:T(8,128)(2,1)}, u32[]{:S(2)}) copy-start(bf16[1,768,2048]{2,1,0:T(8,128)(2,1)} %get-tuple-element.19) | copy-start | bytes 9437188

commit v2 on v1

v2 whole, which is shorter than its diff:
```python
import functools

import jax
import jax.numpy as jnp
from jax import lax
from jax.experimental import pallas as pl
from jax.experimental.pallas import tpu as pltpu
from jax.sharding import PartitionSpec as P

MESH = pl.DeviceIdType.MESH
BF, F32 = jnp.bfloat16, jnp.float32
D, FF, TOK, TOP, SLOTS = 2048, 768, 128, 8, 9
WIDTH = ((640, 768, 640), (640, 640, 768))
START = ((0, 640, 1408), (0, 640, 1280))
TAIL_WIDTH = (640, 768, 768)
TAIL_START = (0, 640, 1280)
HALF = 384
ROWS = 1152
MAIN_A, TAILS = 512, 128


def place():
    node, local = lax.axis_index("node"), lax.axis_index("local")
    return local // 2, (node % 8) // 2, (node // 8) * 2 + local % 2, node % 2


def order(j, x, y, z):
    return ((x, y, z), (y, z, x), (z, x, y))[j]


def device(j, a, b, c, core):
    x, y, z = ((a, b, c), (c, a, b), (b, c, a))[j]
    return ((z // 2) * 8 + y * 2 + core, x * 2 + z % 2)


def canon(j, ref, lead, par, b, c, cols):
    q = (par + b + c) % 2
    every = slice(None)
    if j == 0:
        at = (par, c // 2, c % 2, b // 2, b % 2, every)
    elif j == 1:
        at = (par, b // 2, b % 2, every, q, c // 2)
    else:
        at = (par, every, q, c // 2, c % 2, b // 2)
    return ref.at[lead + at + (every, cols)]


def remote(src, dst, ssem, rsem, dev):
    return pltpu.make_async_remote_copy(
        src_ref=src, dst_ref=dst, send_sem=ssem, recv_sem=rsem, device_id=dev, device_id_type=MESH
    )


def greet(partners):
    barrier = pltpu.get_barrier_semaphore()
    for dev in partners:
        pl.semaphore_signal(barrier, inc=1, device_id=dev, device_id_type=MESH)
    pl.semaphore_wait(barrier, len(partners))


def partners_of(x, y, z, core):
    out = [device(0, x, y, z, 1 - core)]
    for d in (1, 2, 3):
        out.append(device(0, (x + d) % 4, y, z, core))
        out.append(device(0, x, (y + d) % 4, z, core))
        out.append(device(0, x, y, (z + d) % 4, core))
    return out


def iota(shape, dim):
    return lax.broadcasted_iota(jnp.int32, shape, dim)


def tail_perm(j, array):
    row, col = iota((128, 256), 0), iota((128, 256), 1)
    core, x, y, z = row % 2, (row // 2) % 4, (row // 8) % 4, row // 32
    a, b, c = order(j, x, y, z)
    want = c * 64 + b * 16 + array * 8 + a * 2 + core
    return (col == want).astype(F32).astype(BF)


def tail_spread(j, half):
    row, col = iota((256, 128), 0), iota((256, 128), 1)
    c, b, h, a, core = row // 64, (row // 16) % 4, (row // 8) % 2, (row // 2) % 4, row % 2
    x, y, z = ((a, b, c), (c, a, b), (b, c, a))[j]
    return ((col == z * 32 + y * 8 + x * 2 + core) & (h == half)).astype(F32).astype(BF)


def over_rows(left, right):
    return lax.dot_general(left, right, (((0,), (0,)), ((), ())), preferred_element_type=F32)


def across(left, right):
    return lax.dot_general(left, right, (((1,), (1,)), ((), ())), preferred_element_type=F32)


def tile(i):
    return pl.ds(pl.multiple_of(i * 256, 256), 256)


def by_two(refs):
    return tuple(refs[2 * j : 2 * j + 2] for j in range(3))


def kernel(tok, grad, ids, gates, gate_w, up_w, down_w, out, gate_out, up_out, down_out, *rest):
    R, R1, RT, RT1, scr = by_two(rest[:6]), by_two(rest[6:12]), rest[12:15], rest[15:18], rest[18:]
    T, S, R2 = (by_two(scr[6 * i : 6 * i + 6]) for i in range(3))
    ST, FT, ST2, RT2, KEEP = (scr[18 + 3 * i : 21 + 3 * i] for i in range(5))
    PK, OWN, XG, XT, SG, SGT, WG, WU, WD, HID, GG, UG, meta, metas, pos = scr[33:48]
    (ag_s, ag_r, sib_s, sib_r, mag_s, mag_r, msib_s, msib_r, loc, locm,
     p2_s, p2_r, p2t_s, p2t_r, p3_s, p3_r, p3t_s, p3t_r, locp, loct,
     r1_s, r1_r, r1t_s, r1t_r, r2_s, r2_r, r2t_s, r2t_r, l2, l2t,
     ps_s, ps_r, q_s, q_r, wsem, osem, done) = scr[48:]
    x, y, z, core = place()
    axes = [order(j, x, y, z) for j in range(3)]
    sib = device(0, x, y, z, 1 - core)
    weights = ((gate_w, WG), (up_w, WU), (down_w, WD))
    for i, (src, dst) in enumerate(weights):
        pltpu.make_async_copy(src.at[0], dst, wsem.at[i]).start()
    meta[:TOP] = ids[...].astype(F32)
    meta[TOP:] = gates[...].astype(F32)
    greet(partners_of(x, y, z, core))
    ins = (tok, grad)
    sends, early = [], []

    def go(cp, kept=sends):
        cp.start()
        kept.append(cp)

    def got(ref, rsem):
        remote(ref, ref, ag_s.at[0, 0, 0], rsem, sib).wait_recv()

    def landed(ref, sem):
        pltpu.make_async_copy(ref, ref, sem).wait()

    def cols_of(i, j):
        return pl.ds(START[i][j], WIDTH[i][j])

    for j in range(3):
        a, b, c = axes[j]
        for d in (2, 1, 3):
            dev = device(j, (a + d) % 4, b, c, core)
            go(remote(meta, metas.at[j, a, core], mag_s.at[j, d], mag_r.at[j, a], dev))
    for d in (2, 1, 3):
        for j in range(3):
            a, b, c = axes[j]
            dev = device(j, (a + d) % 4, b, c, core)
            for r in range(2):
                src = ins[r].at[:, cols_of(r, j)]
                go(remote(src, T[j][r].at[a, core], ag_s.at[j, d, r], ag_r.at[j, a, r], dev))
    for j in range(3):
        a, b, c = axes[j]
        go(remote(meta, metas.at[j, a, core], msib_s.at[j, a], msib_r.at[j, a], sib))
        pltpu.make_async_copy(meta, metas.at[j, a, core], locm.at[j]).start()
        for r in range(2):
            src = ins[r].at[:, cols_of(r, j)]
            go(remote(src, T[j][r].at[a, core], sib_s.at[j, a, r], sib_r.at[j, a, r], sib))
            pltpu.make_async_copy(src, T[j][r].at[a, core], loc.at[j, r]).start()

    for d in (1, 3, 2):
        for j in range(3):
            s = (axes[j][0] + d) % 4
            m = metas.at[j, s, core]
            got(m, mag_r.at[j, s])
            go(remote(m, m, msib_s.at[j, s], msib_r.at[j, s], sib))
        for j in range(3):
            s = (axes[j][0] + d) % 4
            for r in range(2):
                t = T[j][r].at[s, core]
                got(t, ag_r.at[j, s, r])
                go(remote(t, t, sib_s.at[j, s, r], sib_r.at[j, s, r], sib), early)

    before = (iota((TOK, TOK), 0) < iota((TOK, TOK), 1)).astype(F32).astype(BF)

    def one_hot(j, s, gate, last):
        a = axes[j][0]
        e = iota((16, 1), 0)
        dev = device(j, a, e // 4, e % 4, core)
        expert = (dev[0] * 8 + dev[1]).astype(F32)
        parts = []
        for k in range(2):
            info = metas[j, s, k]
            value = jnp.ones((16, TOK), F32)
            if gate:
                value = jnp.zeros((16, TOK), F32)
                for i in range(TOP):
                    hit = info[i : i + 1, :] == expert
                    value = value + jnp.where(hit, info[TOP + i : TOP + i + 1, :], 0.0)
            at = pos[j, s, k][:, None, :]
            if last:
                hit = (at == 8.0) & (iota((16, 8, TOK), 1) == 2 * s + k)
            else:
                hit = at * 2.0 + k == iota((16, 16, TOK), 1).astype(F32)
            parts.append(jnp.where(hit, value[:, None, :], 0.0).reshape(128 if last else 256, TOK))
        return jnp.concatenate(parts, axis=1).astype(BF)

    def find_slots(j):
        a = axes[j][0]
        e = iota((16, 1), 0)
        dev = device(j, a, e // 4, e % 4, core)
        expert = (dev[0] * 8 + dev[1]).astype(F32)
        for s in range(4):
            for k in range(2):
                info = metas[j, s, k]
                named = jnp.zeros((16, TOK), F32)
                for i in range(TOP):
                    named = named + jnp.where(info[i : i + 1, :] == expert, 1.0, 0.0)
                earlier = jnp.dot(named.astype(BF), before, preferred_element_type=F32)
                pos[j, s, k] = jnp.where(named > 0.5, earlier, -1.0)

    def gather(j, par):
        a, b, c = axes[j]
        for h in range(2):
            s = 2 * h + (par + b + c) % 2
            for r in range(2):
                w = WIDTH[r][j]
                rows = T[j][r][s].reshape(2 * TOK, w)
                main = jnp.dot(one_hot(j, s, r == 1, False), rows, preferred_element_type=F32)
                S[j][r][:, :, par, h] = main.astype(BF).reshape(4, 4, 16, w)

    def gather_tails(j):
        tails = []
        for r in range(2):
            w = WIDTH[r][j]
            rows = jnp.zeros((TAILS, w), F32)
            for s in range(4):
                picked = T[j][r][s].reshape(2 * TOK, w)
                rows = rows + jnp.dot(one_hot(j, s, r == 1, True), picked, preferred_element_type=F32)
            left = START[r][j] - TAIL_START[j]
            right = TAIL_WIDTH[j] - w - left
            rows = [rows]
            if left:
                rows = [jnp.zeros((TAILS, left), F32)] + rows
            if right:
                rows = rows + [jnp.zeros((TAILS, right), F32)]
            tails.append(jnp.concatenate(rows, axis=1).reshape(16, 8, TAIL_WIDTH[j]))
        ST[j][...] = jnp.concatenate(tails, axis=1).astype(BF).reshape(4, 4, 16, TAIL_WIDTH[j])

    def along_b(j, par):
        a, b, c = axes[j]
        for d in (2, 1, 3):
            t = (b + d) % 4
            dev = device(j, a, t, c, core)
            for r in range(2):
                src, dst = S[j][r].at[t, :, par], R[j][r].at[b, :, par]
                go(remote(src, dst, p2_s.at[j, par, d, r], p2_r.at[j, par, b, r], dev))

    def along_c(j, par, d, main):
        a, b, c = axes[j]
        s = (b + d) % 4
        for r in range(2):
            dst = canon(j, XG, (r,), par, s, c, cols_of(r, j))
            for dc in (2, 1, 3):
                t = (c + dc) % 4
                dev = device(j, a, b, t, core)
                go(remote(main[r].at[s, t, par], dst, p3_s.at[j, par, d, dc, r], p3_r.at[j, par, c, s, r], dev))
            pltpu.make_async_copy(main[r].at[s, c, par], dst, locp.at[j, par, d, r]).start()

    def tails_along_b(j):
        a, b, c = axes[j]
        for d in (2, 1, 3):
            t = (b + d) % 4
            dev = device(j, a, t, c, core)
            go(remote(ST[j].at[t], RT[j].at[b], p2t_s.at[j, d], p2t_r.at[j, b], dev))

    def tails_along_c(j, d, tail):
        a, b, c = axes[j]
        s = (b + d) % 4
        for dc in (2, 1, 3):
            t = (c + dc) % 4
            dev = device(j, a, b, t, core)
            go(remote(tail.at[s, t], FT[j].at[c, s], p3t_s.at[j, d, dc], p3t_r.at[j, c, s], dev))
        pltpu.make_async_copy(tail.at[s, c], FT[j].at[c, s], loct.at[j, d]).start()

    def pass_on(par):
        for d in (1, 3, 2):
            for j in range(3):
                s = (axes[j][1] + d) % 4
                for r in range(2):
                    got(R[j][r].at[s, :, par], p2_r.at[j, par, s, r])
                along_c(j, par, d, R[j])

    def pass_tails():
        for d in (1, 3, 2):
            for j in range(3):
                s = (axes[j][1] + d) % 4
                got(RT[j].at[s], p2t_r.at[j, s])
                tails_along_c(j, d, RT[j])

    def arrive(par, offsets):
        for j in range(3):
            a, b, c = axes[j]
            for db in offsets:
                s = (b + db) % 4
                for r in range(2):
                    landed(canon(j, XG, (r,), par, s, c, cols_of(r, j)), locp.at[j, par, db, r])
                    for dc in (1, 2, 3):
                        t = (c + dc) % 4
                        got(canon(j, XG, (r,), par, s, t, cols_of(r, j)), p3_r.at[j, par, t, s, r])

    def arrive_tails():
        for j in range(3):
            a, b, c = axes[j]
            for db in range(4):
                s = (b + db) % 4
                landed(FT[j].at[c, s], loct.at[j, db])
                for dc in (1, 2, 3):
                    t = (c + dc) % 4
                    got(FT[j].at[t, s], p3t_r.at[j, t, s])
            rows = FT[j][...].reshape(256, TAIL_WIDTH[j])
            for r in range(2):
                picked = jnp.dot(tail_perm(j, r), rows, preferred_element_type=F32).astype(BF)
                left = START[r][j] - TAIL_START[j]
                XT[r, :, cols_of(r, j)] = picked[:, left : left + WIDTH[r][j]]

    first, size = (0, MAIN_A + TAILS), (MAIN_A + TAILS, MAIN_A)

    def rows_of(r, par):
        main = XG[r, par].reshape(MAIN_A, D)
        return jnp.concatenate([main, XT[r]], axis=0) if par == 0 else main

    def forward(par):
        span = pl.ds(first[par], size[par])

        def hidden_tile(i, carry):
            cols = tile(i)
            rows = rows_of(0, par)
            gate_pre = jnp.dot(rows, WG[:, cols], preferred_element_type=F32)
            up_pre = jnp.dot(rows, WU[:, cols], preferred_element_type=F32)
            hidden_grad = across(rows_of(1, par), WD[cols, :])
            logistic = jax.nn.sigmoid(gate_pre)
            silu_gate = gate_pre * logistic
            HID[span, cols] = (silu_gate * up_pre).astype(BF)
            UG[span, cols] = (hidden_grad * silu_gate).astype(BF)
            GG[span, cols] = (hidden_grad * up_pre * logistic * (1.0 + gate_pre * (1.0 - logistic))).astype(BF)
            return carry

        lax.fori_loop(0, FF // 256, hidden_tile, 0)

        def slot_tile(i, carry):
            cols = tile(i)
            rows = (across(GG[span, :], WG[cols, :]) + across(UG[span, :], WU[cols, :])).astype(BF)
            SG[par, :, :, :, :, :, :, cols] = rows[:MAIN_A].reshape(2, 2, 2, 2, 2, 16, 256)
            if par == 0:
                SGT[:, cols] = rows[MAIN_A:]
            return carry

        ready = 0
        for j in range(3):
            stop = -(-(START[par][j] + WIDTH[par][j]) // 256)
            lax.fori_loop(ready, stop, slot_tile, 0)
            ready = stop
            back_c(par, j)

    def in_tile(i, carry):
        cols = tile(i)
        parts = [XG[0, 0, :, :, :, :, :, :, cols].reshape(MAIN_A, 256), XT[0, :, cols]]
        rows = jnp.concatenate(parts + [XG[0, 1, :, :, :, :, :, :, cols].reshape(MAIN_A, 256)], axis=0)
        WG[cols, :] = over_rows(rows, GG[...]).astype(BF)
        WU[cols, :] = over_rows(rows, UG[...]).astype(BF)
        return carry

    def down_tile(i, carry):
        cols = tile(i)
        rows = jnp.concatenate([rows_of(1, 0), rows_of(1, 1)], axis=0)
        WD[cols, :] = over_rows(HID[:, cols], rows).astype(BF)
        return carry

    def back_c(par, j):
        a, b, c = axes[j]
        for d in (2, 1, 3):
            t = (c + d) % 4
            dev = device(j, a, b, t, core)
            for bl in range(2):
                if j == 0:
                    at = (par, t // 2, t % 2, slice(None), bl, slice(None))
                elif j == 1:
                    at = (par, slice(None), bl, slice(None), (par + bl + t) % 2, t // 2)
                else:
                    at = (par, slice(None), (par + bl + t) % 2, t // 2, t % 2, slice(None))
                src = SG.at[at + (slice(None), cols_of(par, j))]
                go(remote(src, R1[j][par].at[c, bl], r1_s.at[j, par, d, bl], r1_r.at[j, par, c, bl], dev))
        if par == 0:
            lo, hi = TAIL_START[j], TAIL_START[j] + TAIL_WIDTH[j] - HALF
            rows = jnp.dot(tail_spread(j, 0), SGT[:, lo : lo + HALF], preferred_element_type=F32)
            rows = rows + jnp.dot(tail_spread(j, 1), SGT[:, hi : hi + HALF], preferred_element_type=F32)
            ST2[j][...] = rows.astype(BF).reshape(4, 4, 16, HALF)
            for d in (2, 1, 3):
                t = (c + d) % 4
                dev = device(j, a, b, t, core)
                go(remote(ST2[j].at[t], RT1[j].at[c], r1t_s.at[j, d], r1t_r.at[j, c], dev))
        back_b(j, par, 0, lambda t: canon(j, SG, (), par, t, c, cols_of(par, j)), ST2[j].at[c])

    def back_b(j, par, d, main, tail):
        a, b, c = axes[j]
        s = (c + d) % 4
        for db in (2, 1, 3):
            t = (b + db) % 4
            dev = device(j, a, t, c, core)
            go(remote(main(t), R2[j][par].at[b, s], r2_s.at[j, par, d, db], r2_r.at[j, par, b, s], dev))
            if par == 0:
                go(remote(tail.at[t], RT2[j].at[b, s], r2t_s.at[j, d, db], r2t_r.at[j, b, s], dev))
        pltpu.make_async_copy(main(b), R2[j][par].at[b, s], l2.at[j, par, d]).start()
        if par == 0:
            pltpu.make_async_copy(tail.at[b], RT2[j].at[b, s], l2t.at[j, d]).start()

    def pass_back(par):
        for d in (1, 3, 2):
            for j in range(3):
                s = (axes[j][2] + d) % 4
                for bl in range(2):
                    got(R1[j][par].at[s, bl], r1_r.at[j, par, s, bl])
                if par == 0:
                    got(RT1[j].at[s], r1t_r.at[j, s])

                def main(t, j=j, s=s):
                    if j == 2:
                        return R1[j][par].at[s, t % 2, :, t // 2]
                    return R1[j][par].at[s, t % 2, t // 2]

                back_b(j, par, d, main, RT1[j].at[s])

    def returned(par, j):
        a, b, c = axes[j]
        for dc in (0, 1, 3, 2):
            s = (c + dc) % 4
            landed(R2[j][par].at[b, s], l2.at[j, par, dc])
            for db in (1, 2, 3):
                t = (b + db) % 4
                got(R2[j][par].at[t, s], r2_r.at[j, par, t, s])

    def tails_returned(j):
        a, b, c = axes[j]
        for dc in (0, 1, 3, 2):
            s = (c + dc) % 4
            landed(RT2[j].at[b, s], l2t.at[j, dc])
            for db in (1, 2, 3):
                t = (b + db) % 4
                got(RT2[j].at[t, s], r2t_r.at[j, t, s])

    def prepare(par, j):
        a, b, c = axes[j]
        left, w = START[par][j] - TAIL_START[j], WIDTH[par][j]
        tails = RT2[j][...].reshape(256, HALF)
        for h in range(2):
            s = 2 * h + (par + b + c) % 2
            pick, low, high = [], [], []
            for k in range(2):
                who = (core + k) % 2
                at = pos[j, s, who][:, None, :]
                row = iota((16, 16, TOK), 1)
                hit = at * 2.0 + who.astype(F32) == row.astype(F32)
                pick.append(jnp.where(hit, 1.0, 0.0).reshape(256, TOK))
                hit = (at == 8.0) & (row == 2 * s + who)
                low.append(jnp.where(hit, 1.0, 0.0).reshape(256, TOK))
                hit = (at == 8.0) & (row == 8 + 2 * s + who)
                high.append(jnp.where(hit, 1.0, 0.0).reshape(256, TOK))
            pick, low, high = (jnp.concatenate(p, axis=1).astype(BF) for p in (pick, low, high))
            PK[j, h] = pick
            both = [over_rows(low, tails), over_rows(high, tails)[:, 2 * HALF - TAIL_WIDTH[j] :]]
            KEEP[j][h, :, :w] = jnp.concatenate(both, axis=1)[:, left : left + w]

    def combine(par):
        swaps = []
        for j in range(3):
            returned(par, j)
            w = WIDTH[par][j]
            for h in range(2):
                total = KEEP[j][h, :, :w] + over_rows(PK[j, h], R2[j][par][:, :, h].reshape(256, w))
                KEEP[j][h, :TOK, :w] = total[:TOK]
                T[j][par][h, 0] = total[TOK:].astype(BF)
                mine, theirs = T[j][par].at[h, 0], T[j][par].at[h, 1]
                cp = remote(mine, theirs, ps_s.at[j, 2 * par + h], ps_r.at[j, 2 * par + h], sib)
                cp.start()
                swaps.append(cp)
        for j in range(3):
            a, b, c = axes[j]
            w = WIDTH[par][j]
            for h in range(2):
                s = 2 * h + (par + b + c) % 2
                swaps[2 * j + h].wait_send()
                got(T[j][par].at[h, 1], ps_r.at[j, 2 * par + h])
                total = KEEP[j][h, :TOK, :w] + T[j][par][h, 1].astype(F32)

                @pl.when(s == a)
                def _():
                    OWN[:, cols_of(par, j)] = total

                @pl.when(s != a)
                def _():
                    T[j][par][h, 0] = total.astype(BF)
                    to_line(j, par, h, s).start()

    def to_line(j, par, h, s):
        a, b, c = axes[j]
        dst = T[j][par].at[2 + a // 2, a % 2]
        return remote(T[j][par].at[h, 0], dst, q_s.at[j, 2 * par + h], q_r.at[j, a], device(j, s, b, c, core))

    for j in range(3):
        a, b, c = axes[j]
        landed(metas.at[j, a, core], locm.at[j])
        for s in range(4):
            got(metas.at[j, s, 1 - core], msib_r.at[j, s])
        find_slots(j)
    for j in range(3):
        for r in range(2):
            landed(T[j][r].at[axes[j][0], core], loc.at[j, r])
            for s in range(4):
                got(T[j][r].at[s, 1 - core], sib_r.at[j, s, r])
        gather(j, 0)
        along_b(j, 0)
        along_c(j, 0, 0, S[j])
    for j in range(3):
        gather_tails(j)
        tails_along_b(j)
        tails_along_c(j, 0, ST[j])
    for j in range(3):
        gather(j, 1)
    for cp in early:
        cp.wait_send()
    pl.semaphore_signal(done, inc=1, device_id=sib, device_id_type=MESH)
    pass_on(0)
    pass_tails()
    for j in range(3):
        along_b(j, 1)
        along_c(j, 1, 0, S[j])
    arrive(0, (0, 1, 3, 2))
    arrive_tails()
    for i, (src, dst) in enumerate(weights):
        pltpu.make_async_copy(src.at[0], dst, wsem.at[i]).wait()
    forward(0)
    pass_on(1)
    pass_back(0)
    arrive(1, (0, 1, 3, 2))
    forward(1)
    pl.semaphore_wait(done, 1)
    for j in range(3):
        tails_returned(j)
        prepare(0, j)
    combine(0)
    for j in range(3):
        prepare(1, j)
    pass_back(1)
    lax.fori_loop(0, 8, in_tile, 0)
    pltpu.make_async_copy(WG, gate_out.at[0], osem.at[0]).start()
    pltpu.make_async_copy(WU, up_out.at[0], osem.at[1]).start()
    lax.fori_loop(0, 3, down_tile, 0)
    pltpu.make_async_copy(WD, down_out.at[0], osem.at[2]).start()
    combine(1)
    for m in range(2):

        @pl.when((x + y + z) % 2 == m)
        def _():
            for j in range(3):
                a = axes[j][0]
                total = OWN[:, cols_of(m, j)]
                for d in (1, 3, 2):
                    s = (a + d) % 4
                    part = T[j][m].at[2 + s // 2, s % 2]
                    got(part, q_r.at[j, s])
                    total = total + part[...].astype(F32)
                out[:, cols_of(m, j)] = total.astype(BF)

    for cp in sends:
        cp.wait_send()
    for j in range(3):
        a, b, c = axes[j]
        for i in range(4):
            s = 2 * (i % 2) + (i // 2 + b + c) % 2

            @pl.when(s != a)
            def _():
                to_line(j, i // 2, i % 2, s).wait_send()

    for i, (src, dst) in enumerate(((WG, gate_out), (WU, up_out), (WD, down_out))):
        pltpu.make_async_copy(src, dst.at[0], osem.at[i]).wait()


def run(tokens, out_grad, ids, gates, gate_weight, up_weight, down_weight):
    dma = pltpu.SemaphoreType.DMA
    vm = pltpu.VMEM
    any_spec = pl.BlockSpec(memory_space=pl.ANY)
    vm_spec = pl.BlockSpec(memory_space=pltpu.VMEM)
    shape = jax.ShapeDtypeStruct
    both = [WIDTH[i][j] for j in range(3) for i in range(2)]
    scratch = [vm((4, 2, TOK, w), BF) for w in both]
    scratch += [vm((4, 4, 2, 2, 16, w), BF) for w in both]
    scratch += [vm((4, 4, 2, 16, w), BF) for w in both]
    scratch += [vm((4, 4, 16, w), BF) for w in TAIL_WIDTH] * 2
    scratch += [vm((4, 4, 16, HALF), BF)] * 6
    scratch += [vm((2, 2 * TOK, 768), F32)] * 3
    scratch += [vm((3, 2, 256, 256), BF), vm((TOK, D), F32)]
    scratch += [vm((2, 2, 2, 2, 2, 2, 2, 16, D), BF), vm((2, TAILS, D), BF)]
    scratch += [vm((2, 2, 2, 2, 2, 2, 16, D), BF), vm((TAILS, D), BF)]
    scratch += [vm((D, FF), BF), vm((D, FF), BF), vm((FF, D), BF)] + [vm((ROWS, FF), BF)] * 3
    scratch += [vm((2 * TOP, TOK), F32)] + [vm((3, 4, 2, 16, TOK), F32)] * 2
    scratch += [dma((3, 4, 2))] * 4 + [dma((3, 4))] * 4 + [dma((3, 2)), dma((3,))]
    scratch += [dma((3, 2, 4, 2))] * 2 + [dma((3, 4))] * 2 + [dma((3, 2, 4, 4, 2))] * 2 + [dma((3, 4, 4))] * 2
    scratch += [dma((3, 2, 4, 2)), dma((3, 4))]
    scratch += [dma((3, 2, 4, 2))] * 2 + [dma((3, 4))] * 2 + [dma((3, 2, 4, 4))] * 2 + [dma((3, 4, 4))] * 2
    scratch += [dma((3, 2, 4)), dma((3, 4))]
    scratch += [dma((3, 4))] * 4 + [dma((3,))] * 2 + [pltpu.SemaphoreType.REGULAR]
    outs = [shape((TOK, D), BF), shape((1, D, FF), BF), shape((1, D, FF), BF), shape((1, FF, D), BF)]
    outs += [shape((4, 4, 2, 2, 16, w), BF) for w in both]
    outs += [shape((4, 2, 2, 2, 16, w), BF) for w in both]
    outs += [shape((4, 4, 16, w), BF) for w in TAIL_WIDTH] + [shape((4, 4, 16, HALF), BF)] * 3
    return pl.pallas_call(
        kernel,
        name="experts",
        out_shape=outs,
        in_specs=[any_spec] * 2 + [vm_spec] * 2 + [any_spec] * 3,
        out_specs=[vm_spec] + [any_spec] * 21,
        scratch_shapes=scratch,
        compiler_params=pltpu.CompilerParams(collective_id=0, has_side_effects=True, vmem_limit_bytes=62 << 20),
    )(tokens, out_grad, ids, gates, gate_weight, up_weight, down_weight)[:4]


def body(tokens, out_grad, expert_ids, gates, gate_weight, up_weight, down_weight):
    return tuple(run(tokens, out_grad, expert_ids.T, gates.T, gate_weight, up_weight, down_weight))


def solution(mesh):
    whole = ("node", "local")
    two, three = P(whole, None), P(whole, None, None)
    return jax.shard_map(
        body,
        mesh=mesh,
        in_specs=(two, two, two, two, three, three, three),
        out_specs=(two, three, three, three),
        check_vma=False,
    )
```

time: 191 us -> 190 us (level)
  other arithmetic: 1.97 us -> 0 us
where the time goes in v2:
time: 190 us; the launch traced here: 188 us
  Pallas kernels  177 us (93%)
  local copies, waits for them, and re-layouts  10.5 us (6%)
    pallas_call x1, Pallas kernels, run(): pl.pallas_call(kernel, name='experts', out_shape=outs, in_specs=[any_spec...  177 us
    unnamed x8, local copies, waits for them, and re-layouts  10.5 us

profile of v2, /device:TPU:13, one launch (start us, length us, event | category | flops | bytes accessed | tf_op | source)
XLA Modules:
  0.0 188.4 jit_solution(17887083088841929587)
XLA Ops:
  0.6 177.3 %experts.1 = (bf16[128,2048]{1,0:T(8,128)(2,1)}, bf16[1,2048,768]{2,1,0:T(8,128)(2,1)}, bf16[1,2048,768]{2,1,0:T(8,128)(2,1)}, bf16[1,768,2048]{2,1,0:T(8,128)(2...) custom-call(bf16[128,2048]{1,0:T(8,128)(2,1)} %tok.1, ...), custom_call_target="tpu_custom_call" | custom-call | tf_op jit(solution)/shard_map/experts/pallas_call | solution.py:607
  177.9 1.9 copy.15
  179.8 0.0 copy-start.1
  179.8 3.9 %copy.16 = bf16[1,2048,768]{2,1,0:T(8,128)(2,1)} copy(bf16[1,2048,768]{2,1,0:T(8,128)(2,1)} %get-tuple-element.17) | data formatting | bytes 6291456
  183.7 0.0 copy-done.1
  183.7 0.0 copy-start
  183.7 1.7 copy.17
  185.4 1.4 copy-done
  186.7 1.7 copy.18
Async XLA Ops:
  179.8 3.9 %copy-start.1 = (bf16[1,2048,768]{2,1,0:T(8,128)(2,1)S(1)}, bf16[1,2048,768]{2,1,0:T(8,128)(2,1)}, u32[]{:S(2)}) copy-start(bf16[1,2048,768]{2,1,0:T(8,128)(2,1)} %get-tuple-element.18) | copy-start | bytes 9437188
  183.7 3.0 %copy-start = (bf16[1,768,2048]{2,1,0:T(8,128)(2,1)S(1)}, bf16[1,768,2048]{2,1,0:T(8,128)(2,1)}, u32[]{:S(2)}) copy-start(bf16[1,768,2048]{2,1,0:T(8,128)(2,1)} %get-tuple-element.19) | copy-start | bytes 9437188

commit v3 on v2

--- a/solution.py
+++ b/solution.py
@@ -106,11 +106,12 @@
     R, R1, RT, RT1, scr = by_two(rest[:6]), by_two(rest[6:12]), rest[12:15], rest[15:18], rest[18:]
     T, S, R2 = (by_two(scr[6 * i : 6 * i + 6]) for i in range(3))
     ST, FT, ST2, RT2, KEEP = (scr[18 + 3 * i : 21 + 3 * i] for i in range(5))
-    PK, OWN, XG, XT, SG, SGT, WG, WU, WD, HID, GG, UG, meta, metas, pos = scr[33:48]
+    PK, OWN, XG, XT, SG, SGT, HID, GG, UG, meta, metas, pos = scr[33:45]
     (ag_s, ag_r, sib_s, sib_r, mag_s, mag_r, msib_s, msib_r, loc, locm,
      p2_s, p2_r, p2t_s, p2t_r, p3_s, p3_r, p3t_s, p3t_r, locp, loct,
      r1_s, r1_r, r1t_s, r1t_r, r2_s, r2_r, r2t_s, r2t_r, l2, l2t,
-     ps_s, ps_r, q_s, q_r, wsem, osem, done) = scr[48:]
+     ps_s, ps_r, q_s, q_r, wsem, done) = scr[45:]
+    WG, WU, WD = gate_out.at[0], up_out.at[0], down_out.at[0]
     x, y, z, core = place()
     axes = [order(j, x, y, z) for j in range(3)]
     sib = device(0, x, y, z, 1 - core)
@@ -141,13 +142,37 @@
         for d in (2, 1, 3):
             dev = device(j, (a + d) % 4, b, c, core)
             go(remote(meta, metas.at[j, a, core], mag_s.at[j, d], mag_r.at[j, a], dev))
-    for d in (2, 1, 3):
-        for j in range(3):
-            a, b, c = axes[j]
-            dev = device(j, (a + d) % 4, b, c, core)
-            for r in range(2):
+    def to_lines(r):
+        for d in (1, 3):
+            for j in range(3):
+                a, b, c = axes[j]
+                dev = device(j, (a + d) % 4, b, c, core)
                 src = ins[r].at[:, cols_of(r, j)]
                 go(remote(src, T[j][r].at[a, core], ag_s.at[j, d, r], ag_r.at[j, a, r], dev))
+
+    def metas_across(d):
+        for j in range(3):
+            s = (axes[j][0] + d) % 4
+            m = metas.at[j, s, core]
+            got(m, mag_r.at[j, s])
+            go(remote(m, m, msib_s.at[j, s], msib_r.at[j, s], sib))
+
+    def rows_across(d, r):
+        for j in range(3):
+            s = (axes[j][0] + d) % 4
+            t = T[j][r].at[s, core]
+            got(t, ag_r.at[j, s, r])
+            go(remote(t, t, sib_s.at[j, s, r], sib_r.at[j, s, r], sib), early)
+
+    def second_hop(r):
+        for j in range(3):
+            a, b, c = axes[j]
+            way = 1 - 2 * core
+            t = T[j][r].at[(a - way) % 4, core]
+            dev = device(j, (a + way) % 4, b, c, core)
+            go(remote(t, t, ag_s.at[j, 2, r], ag_r.at[j, (a - way) % 4, r], dev), early)
+
+    to_lines(0)
     for j in range(3):
         a, b, c = axes[j]
         go(remote(meta, metas.at[j, a, core], msib_s.at[j, a], msib_r.at[j, a], sib))
@@ -156,19 +181,13 @@
             src = ins[r].at[:, cols_of(r, j)]
             go(remote(src, T[j][r].at[a, core], sib_s.at[j, a, r], sib_r.at[j, a, r], sib))
             pltpu.make_async_copy(src, T[j][r].at[a, core], loc.at[j, r]).start()
-
-    for d in (1, 3, 2):
-        for j in range(3):
-            s = (axes[j][0] + d) % 4
-            m = metas.at[j, s, core]
-            got(m, mag_r.at[j, s])
-            go(remote(m, m, msib_s.at[j, s], msib_r.at[j, s], sib))
-        for j in range(3):
-            s = (axes[j][0] + d) % 4
-            for r in range(2):
-                t = T[j][r].at[s, core]
-                got(t, ag_r.at[j, s, r])
-                go(remote(t, t, sib_s.at[j, s, r], sib_r.at[j, s, r], sib), early)
+    for d in (1, 3):
+        metas_across(d)
+        rows_across(d, 0)
+    second_hop(0)
+    to_lines(1)
+    metas_across(2)
+    rows_across(2, 0)
 
     before = (iota((TOK, TOK), 0) < iota((TOK, TOK), 1)).astype(F32).astype(BF)
 
@@ -208,15 +227,14 @@
                 earlier = jnp.dot(named.astype(BF), before, preferred_element_type=F32)
                 pos[j, s, k] = jnp.where(named > 0.5, earlier, -1.0)
 
-    def gather(j, par):
-        a, b, c = axes[j]
+    def gather(j, par, r):
+        a, b, c = axes[j]
+        w = WIDTH[r][j]
         for h in range(2):
             s = 2 * h + (par + b + c) % 2
-            for r in range(2):
-                w = WIDTH[r][j]
-                rows = T[j][r][s].reshape(2 * TOK, w)
-                main = jnp.dot(one_hot(j, s, r == 1, False), rows, preferred_element_type=F32)
-                S[j][r][:, :, par, h] = main.astype(BF).reshape(4, 4, 16, w)
+            rows = T[j][r][s].reshape(2 * TOK, w)
+            main = jnp.dot(one_hot(j, s, r == 1, False), rows, preferred_element_type=F32)
+            S[j][r][:, :, par, h] = main.astype(BF).reshape(4, 4, 16, w)
 
     def gather_tails(j):
         tails = []
@@ -236,25 +254,27 @@
             tails.append(jnp.concatenate(rows, axis=1).reshape(16, 8, TAIL_WIDTH[j]))
         ST[j][...] = jnp.concatenate(tails, axis=1).astype(BF).reshape(4, 4, 16, TAIL_WIDTH[j])
 
-    def along_b(j, par):
+    def along_b(j, par, r):
         a, b, c = axes[j]
         for d in (2, 1, 3):
             t = (b + d) % 4
             dev = device(j, a, t, c, core)
-            for r in range(2):
-                src, dst = S[j][r].at[t, :, par], R[j][r].at[b, :, par]
-                go(remote(src, dst, p2_s.at[j, par, d, r], p2_r.at[j, par, b, r], dev))
-
-    def along_c(j, par, d, main):
+            src, dst = S[j][r].at[t, :, par], R[j][r].at[b, :, par]
+            go(remote(src, dst, p2_s.at[j, par, d, r], p2_r.at[j, par, b, r], dev))
+
+    def along_c(j, par, d, r, main):
         a, b, c = axes[j]
         s = (b + d) % 4
-        for r in range(2):
-            dst = canon(j, XG, (r,), par, s, c, cols_of(r, j))
-            for dc in (2, 1, 3):
-                t = (c + dc) % 4
-                dev = device(j, a, b, t, core)
-                go(remote(main[r].at[s, t, par], dst, p3_s.at[j, par, d, dc, r], p3_r.at[j, par, c, s, r], dev))
-            pltpu.make_async_copy(main[r].at[s, c, par], dst, locp.at[j, par, d, r]).start()
+        dst = canon(j, XG, (r,), par, s, c, cols_of(r, j))
+        for dc in (2, 1, 3):
+            t = (c + dc) % 4
+            dev = device(j, a, b, t, core)
+            go(remote(main.at[s, t, par], dst, p3_s.at[j, par, d, dc, r], p3_r.at[j, par, c, s, r], dev))
+        pltpu.make_async_copy(main.at[s, c, par], dst, locp.at[j, par, d, r]).start()
+
+    def depart(j, par, r):
+        along_b(j, par, r)
+        along_c(j, par, 0, r, S[j][r])
 
     def tails_along_b(j):
         a, b, c = axes[j]
@@ -272,13 +292,12 @@
             go(remote(tail.at[s, t], FT[j].at[c, s], p3t_s.at[j, d, dc], p3t_r.at[j, c, s], dev))
         pltpu.make_async_copy(tail.at[s, c], FT[j].at[c, s], loct.at[j, d]).start()
 
-    def pass_on(par):
+    def pass_on(par, r):
         for d in (1, 3, 2):
             for j in range(3):
                 s = (axes[j][1] + d) % 4
-                for r in range(2):
-                    got(R[j][r].at[s, :, par], p2_r.at[j, par, s, r])
-                along_c(j, par, d, R[j])
+                got(R[j][r].at[s, :, par], p2_r.at[j, par, s, r])
+                along_c(j, par, d, r, R[j][r])
 
     def pass_tails():
         for d in (1, 3, 2):
@@ -287,16 +306,15 @@
                 got(RT[j].at[s], p2t_r.at[j, s])
                 tails_along_c(j, d, RT[j])
 
-    def arrive(par, offsets):
+    def arrive(par, r):
         for j in range(3):
             a, b, c = axes[j]
-            for db in offsets:
+            for db in (0, 1, 3, 2):
                 s = (b + db) % 4
-                for r in range(2):
-                    landed(canon(j, XG, (r,), par, s, c, cols_of(r, j)), locp.at[j, par, db, r])
-                    for dc in (1, 2, 3):
-                        t = (c + dc) % 4
-                        got(canon(j, XG, (r,), par, s, t, cols_of(r, j)), p3_r.at[j, par, t, s, r])
+                landed(canon(j, XG, (r,), par, s, c, cols_of(r, j)), locp.at[j, par, db, r])
+                for dc in (1, 2, 3):
+                    t = (c + dc) % 4
+                    got(canon(j, XG, (r,), par, s, t, cols_of(r, j)), p3_r.at[j, par, t, s, r])
 
     def arrive_tails():
         for j in range(3):
@@ -319,14 +337,28 @@
         main = XG[r, par].reshape(MAIN_A, D)
         return jnp.concatenate([main, XT[r]], axis=0) if par == 0 else main
 
+    def before_hidden():
+        def tile_of(i, carry):
+            cols = tile(i)
+            rows = rows_of(0, 1)
+            KEEP[0][:, :, cols] = jnp.dot(rows, WG[:, cols], preferred_element_type=F32).reshape(2, 256, 256)
+            KEEP[1][:, :, cols] = jnp.dot(rows, WU[:, cols], preferred_element_type=F32).reshape(2, 256, 256)
+            return carry
+
+        lax.fori_loop(0, FF // 256, tile_of, 0)
+
     def forward(par):
         span = pl.ds(first[par], size[par])
 
         def hidden_tile(i, carry):
             cols = tile(i)
-            rows = rows_of(0, par)
-            gate_pre = jnp.dot(rows, WG[:, cols], preferred_element_type=F32)
-            up_pre = jnp.dot(rows, WU[:, cols], preferred_element_type=F32)
+            if par == 0:
+                rows = rows_of(0, par)
+                gate_pre = jnp.dot(rows, WG[:, cols], preferred_element_type=F32)
+                up_pre = jnp.dot(rows, WU[:, cols], preferred_element_type=F32)
+            else:
+                gate_pre = KEEP[0][:, :, cols].reshape(MAIN_A, 256)
+                up_pre = KEEP[1][:, :, cols].reshape(MAIN_A, 256)
             hidden_grad = across(rows_of(1, par), WD[cols, :])
             logistic = jax.nn.sigmoid(gate_pre)
             silu_gate = gate_pre * logistic
@@ -502,36 +534,51 @@
         for s in range(4):
             got(metas.at[j, s, 1 - core], msib_r.at[j, s])
         find_slots(j)
-    for j in range(3):
-        for r in range(2):
-            landed(T[j][r].at[axes[j][0], core], loc.at[j, r])
-            for s in range(4):
-                got(T[j][r].at[s, 1 - core], sib_r.at[j, s, r])
-        gather(j, 0)
-        along_b(j, 0)
-        along_c(j, 0, 0, S[j])
+    def complete(j, r):
+        landed(T[j][r].at[axes[j][0], core], loc.at[j, r])
+        for s in range(4):
+            got(T[j][r].at[s, 1 - core], sib_r.at[j, s, r])
+
+    for j in range(3):
+        complete(j, 0)
+        gather(j, 0, 0)
+        depart(j, 0, 0)
+    for d in (1, 3):
+        rows_across(d, 1)
+    second_hop(1)
+    pass_on(0, 0)
+    rows_across(2, 1)
+    for j in range(3):
+        complete(j, 1)
+        gather(j, 0, 1)
+        depart(j, 0, 1)
     for j in range(3):
         gather_tails(j)
         tails_along_b(j)
         tails_along_c(j, 0, ST[j])
     for j in range(3):
-        gather(j, 1)
+        for r in range(2):
+            gather(j, 1, r)
     for cp in early:
         cp.wait_send()
     pl.semaphore_signal(done, inc=1, device_id=sib, device_id_type=MESH)
-    pass_on(0)
+    pass_on(0, 1)
     pass_tails()
-    for j in range(3):
-        along_b(j, 1)
-        along_c(j, 1, 0, S[j])
-    arrive(0, (0, 1, 3, 2))
+    for r in range(2):
+        for j in range(3):
+            depart(j, 1, r)
+    arrive(0, 0)
+    arrive(0, 1)
     arrive_tails()
     for i, (src, dst) in enumerate(weights):
         pltpu.make_async_copy(src.at[0], dst, wsem.at[i]).wait()
     forward(0)
-    pass_on(1)
+    pass_on(1, 0)
+    pass_on(1, 1)
     pass_back(0)
-    arrive(1, (0, 1, 3, 2))
+    arrive(1, 0)
+    before_hidden()
+    arrive(1, 1)
     forward(1)
     pl.semaphore_wait(done, 1)
     for j in range(3):
@@ -542,10 +589,7 @@
         prepare(1, j)
     pass_back(1)
     lax.fori_loop(0, 8, in_tile, 0)
-    pltpu.make_async_copy(WG, gate_out.at[0], osem.at[0]).start()
-    pltpu.make_async_copy(WU, up_out.at[0], osem.at[1]).start()
     lax.fori_loop(0, 3, down_tile, 0)
-    pltpu.make_async_copy(WD, down_out.at[0], osem.at[2]).start()
     combine(1)
     for m in range(2):
 
@@ -571,9 +615,6 @@
             @pl.when(s != a)
             def _():
                 to_line(j, i // 2, i % 2, s).wait_send()
-
-    for i, (src, dst) in enumerate(((WG, gate_out), (WU, up_out), (WD, down_out))):
-        pltpu.make_async_copy(src, dst.at[0], osem.at[i]).wait()
 
 
 def run(tokens, out_grad, ids, gates, gate_weight, up_weight, down_weight):
@@ -592,15 +633,15 @@
     scratch += [vm((3, 2, 256, 256), BF), vm((TOK, D), F32)]
     scratch += [vm((2, 2, 2, 2, 2, 2, 2, 16, D), BF), vm((2, TAILS, D), BF)]
     scratch += [vm((2, 2, 2, 2, 2, 2, 16, D), BF), vm((TAILS, D), BF)]
-    scratch += [vm((D, FF), BF), vm((D, FF), BF), vm((FF, D), BF)] + [vm((ROWS, FF), BF)] * 3
+    scratch += [vm((ROWS, FF), BF)] * 3
     scratch += [vm((2 * TOP, TOK), F32)] + [vm((3, 4, 2, 16, TOK), F32)] * 2
     scratch += [dma((3, 4, 2))] * 4 + [dma((3, 4))] * 4 + [dma((3, 2)), dma((3,))]
     scratch += [dma((3, 2, 4, 2))] * 2 + [dma((3, 4))] * 2 + [dma((3, 2, 4, 4, 2))] * 2 + [dma((3, 4, 4))] * 2
     scratch += [dma((3, 2, 4, 2)), dma((3, 4))]
     scratch += [dma((3, 2, 4, 2))] * 2 + [dma((3, 4))] * 2 + [dma((3, 2, 4, 4))] * 2 + [dma((3, 4, 4))] * 2
     scratch += [dma((3, 2, 4)), dma((3, 4))]
-    scratch += [dma((3, 4))] * 4 + [dma((3,))] * 2 + [pltpu.SemaphoreType.REGULAR]
-    outs = [shape((TOK, D), BF), shape((1, D, FF), BF), shape((1, D, FF), BF), shape((1, FF, D), BF)]
+    scratch += [dma((3, 4))] * 4 + [dma((3,))] + [pltpu.SemaphoreType.REGULAR]
+    outs = [vm((TOK, D), BF), vm((1, D, FF), BF), vm((1, D, FF), BF), vm((1, FF, D), BF)]
     outs += [shape((4, 4, 2, 2, 16, w), BF) for w in both]
     outs += [shape((4, 2, 2, 2, 16, w), BF) for w in both]
     outs += [shape((4, 4, 16, w), BF) for w in TAIL_WIDTH] + [shape((4, 4, 16, HALF), BF)] * 3
@@ -609,9 +650,9 @@
         name="experts",
         out_shape=outs,
         in_specs=[any_spec] * 2 + [vm_spec] * 2 + [any_spec] * 3,
-        out_specs=[vm_spec] + [any_spec] * 21,
+        out_specs=[vm_spec] * 4 + [any_spec] * 18,
         scratch_shapes=scratch,
-        compiler_params=pltpu.CompilerParams(collective_id=0, has_side_effects=True, vmem_limit_bytes=62 << 20),
+        compiler_params=pltpu.CompilerParams(collective_id=0, has_side_effects=True, vmem_limit_bytes=52 << 20),
     )(tokens, out_grad, ids, gates, gate_weight, up_weight, down_weight)[:4]
 
 

time: 190 us -> 177 us (0.932)
  Pallas kernels: 177 us -> 169 us
  local copies, waits for them, and re-layouts: 10.5 us -> 5.79 us
    pallas_call x1, Pallas kernels: 177 us -> 169 us  [run(): pl.pallas_call(kernel, name='experts', out_shape=outs, in_specs=[any_spec...]
    unnamed x8 -> x4, local copies, waits for them, and re-layouts: 10.5 us -> 5.79 us
where the time goes in v3:
time: 177 us; the launch traced here: 176 us
  Pallas kernels  169 us (95%)
  local copies, waits for them, and re-layouts  5.79 us (3%)
    pallas_call x1, Pallas kernels, run(): pl.pallas_call(kernel, name='experts', out_shape=outs, in_specs=[any_spec...  169 us
    unnamed x4, local copies, waits for them, and re-layouts  5.79 us

profile of v3, /device:TPU:13, one launch (start us, length us, event | category | flops | bytes accessed | tf_op | source)
XLA Modules:
  0.0 175.8 jit_solution(6443002001912101520)
XLA Ops:
  0.6 169.4 %experts.1 = (bf16[128,2048]{1,0:T(8,128)(2,1)S(1)}, bf16[1,2048,768]{2,1,0:T(8,128)(2,1)S(1)}, bf16[1,2048,768]{2,1,0:T(8,128)(2,1)S(1)}, bf16[1,768,2048]{2,1,...) custom-call(bf16[128,2048]{1,0:T(8,128)(2,1)} %tok.1, ...), custom_call_target="tpu_custom_call" | custom-call | tf_op jit(solution)/shard_map/experts/pallas_call | solution.py:648
  170.0 0.8 copy.15
  170.8 1.7 copy.16
  172.5 1.7 copy.17
  174.1 1.7 copy.18

commit v4 on v3

--- a/solution.py
+++ b/solution.py
@@ -128,6 +128,11 @@
         cp.start()
         kept.append(cp)
 
+    def drain(count):
+        for cp in sends[:count]:
+            cp.wait_send()
+        del sends[:count]
+
     def got(ref, rsem):
         remote(ref, ref, ag_s.at[0, 0, 0], rsem, sib).wait_recv()
 
@@ -347,7 +352,7 @@
 
         lax.fori_loop(0, FF // 256, tile_of, 0)
 
-    def forward(par):
+    def forward(par, meanwhile=lambda: None):
         span = pl.ds(first[par], size[par])
 
         def hidden_tile(i, carry):
@@ -368,6 +373,7 @@
             return carry
 
         lax.fori_loop(0, FF // 256, hidden_tile, 0)
+        meanwhile()
 
         def slot_tile(i, carry):
             cols = tile(i)
@@ -492,7 +498,7 @@
             both = [over_rows(low, tails), over_rows(high, tails)[:, 2 * HALF - TAIL_WIDTH[j] :]]
             KEEP[j][h, :, :w] = jnp.concatenate(both, axis=1)[:, left : left + w]
 
-    def combine(par):
+    def combine(par, meanwhile):
         swaps = []
         for j in range(3):
             returned(par, j)
@@ -505,6 +511,7 @@
                 cp = remote(mine, theirs, ps_s.at[j, 2 * par + h], ps_r.at[j, 2 * par + h], sib)
                 cp.start()
                 swaps.append(cp)
+        meanwhile()
         for j in range(3):
             a, b, c = axes[j]
             w = WIDTH[par][j]
@@ -533,13 +540,13 @@
         landed(metas.at[j, a, core], locm.at[j])
         for s in range(4):
             got(metas.at[j, s, 1 - core], msib_r.at[j, s])
-        find_slots(j)
     def complete(j, r):
         landed(T[j][r].at[axes[j][0], core], loc.at[j, r])
         for s in range(4):
             got(T[j][r].at[s, 1 - core], sib_r.at[j, s, r])
 
     for j in range(3):
+        find_slots(j)
         complete(j, 0)
         gather(j, 0, 0)
         depart(j, 0, 0)
@@ -572,9 +579,9 @@
     arrive_tails()
     for i, (src, dst) in enumerate(weights):
         pltpu.make_async_copy(src.at[0], dst, wsem.at[i]).wait()
-    forward(0)
-    pass_on(1, 0)
+    forward(0, lambda: pass_on(1, 0))
     pass_on(1, 1)
+    old = len(sends)
     pass_back(0)
     arrive(1, 0)
     before_hidden()
@@ -584,13 +591,17 @@
     for j in range(3):
         tails_returned(j)
         prepare(0, j)
-    combine(0)
+    combine(0, lambda: lax.fori_loop(0, 2, in_tile, 0))
     for j in range(3):
         prepare(1, j)
+    drain(old)
+    lax.fori_loop(2, 4, in_tile, 0)
+    old = len(sends)
     pass_back(1)
-    lax.fori_loop(0, 8, in_tile, 0)
+    lax.fori_loop(4, 8, in_tile, 0)
     lax.fori_loop(0, 3, down_tile, 0)
-    combine(1)
+    drain(old)
+    combine(1, lambda: drain(len(sends)))
     for m in range(2):
 
         @pl.when((x + y + z) % 2 == m)
@@ -605,8 +616,6 @@
                     total = total + part[...].astype(F32)
                 out[:, cols_of(m, j)] = total.astype(BF)
 
-    for cp in sends:
-        cp.wait_send()
     for j in range(3):
         a, b, c = axes[j]
         for i in range(4):

time: 177 us -> 171 us (0.966)
  Pallas kernels: 169 us -> 163 us
    pallas_call x1, Pallas kernels: 169 us -> 163 us  [run(): pl.pallas_call(kernel, name='experts', out_shape=outs, in_specs=[any_spec...]
where the time goes in v4:
time: 171 us; the launch traced here: 170 us
  Pallas kernels  163 us (95%)
  local copies, waits for them, and re-layouts  5.79 us (3%)
    pallas_call x1, Pallas kernels, run(): pl.pallas_call(kernel, name='experts', out_shape=outs, in_specs=[any_spec...  163 us
    unnamed x4, local copies, waits for them, and re-layouts  5.79 us

profile of v4, /device:TPU:13, one launch (start us, length us, event | category | flops | bytes accessed | tf_op | source)
XLA Modules:
  0.0 169.8 jit_solution(9489252047468279505)
XLA Ops:
  0.6 163.3 %experts.1 = (bf16[128,2048]{1,0:T(8,128)(2,1)S(1)}, bf16[1,2048,768]{2,1,0:T(8,128)(2,1)S(1)}, bf16[1,2048,768]{2,1,0:T(8,128)(2,1)S(1)}, bf16[1,768,2048]{2,1,...) custom-call(bf16[128,2048]{1,0:T(8,128)(2,1)} %tok.1, ...), custom_call_target="tpu_custom_call" | custom-call | tf_op jit(solution)/shard_map/experts/pallas_call | solution.py:657
  164.0 0.8 copy.15
  164.8 1.7 copy.16
  166.4 1.7 copy.17
  168.1 1.7 copy.18

commit v5 on v4

--- a/solution.py
+++ b/solution.py
@@ -352,7 +352,7 @@
 
         lax.fori_loop(0, FF // 256, tile_of, 0)
 
-    def forward(par, meanwhile=lambda: None):
+    def forward(par, meanwhile=lambda: None, later=lambda: None):
         span = pl.ds(first[par], size[par])
 
         def hidden_tile(i, carry):
@@ -389,6 +389,8 @@
             lax.fori_loop(ready, stop, slot_tile, 0)
             ready = stop
             back_c(par, j)
+            if j == 0:
+                later()
 
     def in_tile(i, carry):
         cols = tile(i)
@@ -579,8 +581,7 @@
     arrive_tails()
     for i, (src, dst) in enumerate(weights):
         pltpu.make_async_copy(src.at[0], dst, wsem.at[i]).wait()
-    forward(0, lambda: pass_on(1, 0))
-    pass_on(1, 1)
+    forward(0, lambda: pass_on(1, 0), lambda: pass_on(1, 1))
     old = len(sends)
     pass_back(0)
     arrive(1, 0)

time: 171 us -> 173 us (1.012)
  Pallas kernels: 163 us -> 165 us
    pallas_call x1, Pallas kernels: 163 us -> 165 us  [run(): pl.pallas_call(kernel, name='experts', out_shape=outs, in_specs=[any_spec...]
where the time goes in v5:
time: 173 us; the launch traced here: 172 us
  Pallas kernels  165 us (95%)
  local copies, waits for them, and re-layouts  5.79 us (3%)
    pallas_call x1, Pallas kernels, run(): pl.pallas_call(kernel, name='experts', out_shape=outs, in_specs=[any_spec...  165 us
    unnamed x4, local copies, waits for them, and re-layouts  5.79 us

profile of v5, /device:TPU:13, one launch (start us, length us, event | category | flops | bytes accessed | tf_op | source)
XLA Modules:
  0.0 171.6 jit_solution(5781409849000193719)
XLA Ops:
  0.6 165.1 %experts.1 = (bf16[128,2048]{1,0:T(8,128)(2,1)S(1)}, bf16[1,2048,768]{2,1,0:T(8,128)(2,1)S(1)}, bf16[1,2048,768]{2,1,0:T(8,128)(2,1)S(1)}, bf16[1,768,2048]{2,1,...) custom-call(bf16[128,2048]{1,0:T(8,128)(2,1)} %tok.1, ...), custom_call_target="tpu_custom_call" | custom-call | tf_op jit(solution)/shard_map/experts/pallas_call | solution.py:658
  165.8 0.8 copy.15
  166.6 1.7 copy.16
  168.2 1.7 copy.17
  169.9 1.7 copy.18
